TPU v7x, 512 devices: a whole 4x8x8 slice. The times are simulated.
512 devices in a mesh: tile: 128 (over y, z, x_hi), date: 4 (over x_lo, core).
Axes of the slice: x: 4 (x_hi: 2, x_lo: 2; x = x_hi * 2 + x_lo), y: 8, z: 8, core: 2. Of those that a mesh axis runs over, the one named last changes fastest.
Arguments:
- inputs: bfloat16 [128, 4, 12, 8, 8, 192], P('tile', 'date'), may hold values from -74 to 74
- state: bfloat16 [128, 4, 12, 8, 8, 192], P('tile', 'date'), may hold values from -1 to 1
- cotangent: bfloat16 [128, 4, 12, 8, 8, 192], P('tile', 'date'), may hold values from -6 to 6
- adjacency: int32 [12, 4, 2], replicated, may hold values from 0 to 11, as said below
- taps: bfloat16 [2, 3, 192], replicated, may hold values from -3.5 to 3.5
- gain: bfloat16 [192], replicated, may hold values from 0.099609375 to 1.8984375
- w_up: bfloat16 [192, 768], replicated, may hold values from -0.4375 to 0.4375
- b_up: bfloat16 [768], replicated, may hold values from -3 to 3
- w_down: bfloat16 [768, 192], replicated, may hold values from -0.21875 to 0.21875
- b_down: bfloat16 [192], replicated, may hold values from -3 to 3
- w_gates: bfloat16 [384, 384], replicated, may hold values from -0.3125 to 0.3125
- b_gates: bfloat16 [384], replicated, may hold values from -3 to 3
- w_cand: bfloat16 [384, 192], replicated, may hold values from -0.3125 to 0.3125
- b_cand: bfloat16 [192], replicated, may hold values from -3 to 3
Outputs:
- new_state: bfloat16 [128, 4, 12, 8, 8, 192], P('tile', 'date')
- grad_input: bfloat16 [128, 4, 12, 8, 8, 192], P('tile', 'date')
- grad_taps: bfloat16 [2, 3, 192], replicated
- grad_gain: bfloat16 [192], replicated
- grad_up: bfloat16 [192, 768], replicated
- grad_bup: bfloat16 [768], replicated
- grad_down: bfloat16 [768, 192], replicated
- grad_bdown: bfloat16 [192], replicated
- grad_gates: bfloat16 [384, 384], replicated
- grad_bgates: bfloat16 [384], replicated
- grad_cand: bfloat16 [384, 192], replicated
- grad_bcand: bfloat16 [192], replicated
Inputs may be any that keep to these rules, and one draw needn't show every extreme that they name: adjacency[f, e] = (n, k): edge e of face f borders edge k of face n, pixel a along e lying beside pixel a along k; k is the opposite edge (e + 2) mod 4, or else the first row is joined to the first column, or the last column to the last row; the pairing is symmetric, and the faces are those of the HEALPix base in some numbering.
All inputs are finite; a program needn't handle non-finite values.
Results may differ from a plain program's by a relative error of at most 0.012.
Values may be sent and summed in bfloat16 or wider, within the bound.
A program may use at most 64 MiB of HBM per device.

v0:
```python
import jax
import jax.numpy as jnp
from jax import lax
from jax.sharding import PartitionSpec as P

EPSILON = 1e-06


def passed_along(value, axis, steps):
    count = lax.axis_size(axis)
    pairs = [(source, (source + steps) % count) for source in range(count)]
    return lax.ppermute(value, axis, pairs)


def swapped(value, axis, stride):
    mask = 2**stride
    pairs = [(source, source ^ mask) for source in range(lax.axis_size(axis))]
    return lax.ppermute(value, axis, pairs)


def normalize(values):
    average = jnp.mean(values, axis=-1, keepdims=True)
    centred = values - average
    inv_scale = lax.rsqrt(jnp.mean(centred * centred, axis=-1, keepdims=True) + EPSILON)
    return (centred * inv_scale, inv_scale)


def normalize_back(d_standard, standard, inv_scale):
    first_mean = jnp.mean(d_standard, axis=-1, keepdims=True)
    second_mean = jnp.mean(d_standard * standard, axis=-1, keepdims=True)
    return inv_scale * (d_standard - first_mean - standard * second_mean)


def cell_step(
    inputs_rows,
    state_rows,
    cot_rows,
    second,
    gain,
    w_up,
    b_up,
    w_down,
    b_down,
    w_gates,
    b_gates,
    w_cand,
    b_cand,
):
    channels = inputs_rows.shape[1]
    standard, inv_scale = normalize(second)
    normed = (standard * gain.astype(jnp.float32)).astype(jnp.bfloat16)
    pre_up = jnp.dot(normed, w_up, preferred_element_type=jnp.float32) + b_up.astype(jnp.float32)
    hidden = jax.nn.gelu(pre_up).astype(jnp.bfloat16)
    mixed_out = (
        inputs_rows.astype(jnp.float32)
        + jnp.dot(hidden, w_down, preferred_element_type=jnp.float32)
        + b_down.astype(jnp.float32)
    ).astype(jnp.bfloat16)
    joined = jnp.concatenate([mixed_out, state_rows], axis=1)
    gate_pre = jnp.dot(joined, w_gates, preferred_element_type=jnp.float32) + b_gates.astype(
        jnp.float32
    )
    update = jax.nn.sigmoid(gate_pre[:, :channels])
    reset_gate = jax.nn.sigmoid(gate_pre[:, channels:])
    prior_state = state_rows.astype(jnp.float32)
    reset_state = (reset_gate * prior_state).astype(jnp.bfloat16)
    joined_reset = jnp.concatenate([mixed_out, reset_state], axis=1)
    candidate = jnp.tanh(
        jnp.dot(joined_reset, w_cand, preferred_element_type=jnp.float32)
        + b_cand.astype(jnp.float32)
    )
    new_state = lax.optimization_barrier(
        ((1.0 - update) * candidate + update * prior_state).astype(jnp.bfloat16)
    )
    upstream = cot_rows.astype(jnp.float32)
    d_cand = (upstream * (1.0 - update) * (1.0 - candidate * candidate)).astype(jnp.bfloat16)
    d_joined_reset = jnp.dot(d_cand, w_cand.T, preferred_element_type=jnp.float32)
    d_update = upstream * (prior_state - candidate) * update * (1.0 - update)
    d_reset = d_joined_reset[:, channels:] * prior_state * reset_gate * (1.0 - reset_gate)
    d_gate = jnp.concatenate([d_update, d_reset], axis=1).astype(jnp.bfloat16)
    d_joined = jnp.dot(d_gate, w_gates.T, preferred_element_type=jnp.float32)
    d_mixed = lax.optimization_barrier(
        (d_joined_reset[:, :channels] + d_joined[:, :channels]).astype(jnp.bfloat16)
    )
    d_hidden = jnp.dot(d_mixed, w_down.T, preferred_element_type=jnp.float32)
    gelu_back = jax.vjp(jax.nn.gelu, pre_up)[1]
    d_pre_up = gelu_back(d_hidden)[0].astype(jnp.bfloat16)
    d_normed = jnp.dot(d_pre_up, w_up.T, preferred_element_type=jnp.float32)
    d_second = lax.optimization_barrier(
        normalize_back(d_normed * gain.astype(jnp.float32), standard, inv_scale).astype(
            jnp.bfloat16
        )
    )
    grad_sums = (
        jnp.sum(d_normed * standard, axis=0),
        jnp.dot(normed.T, d_pre_up, preferred_element_type=jnp.float32),
        jnp.sum(d_pre_up.astype(jnp.float32), axis=0),
        jnp.dot(hidden.T, d_mixed, preferred_element_type=jnp.float32),
        jnp.sum(d_mixed.astype(jnp.float32), axis=0),
        jnp.dot(joined.T, d_gate, preferred_element_type=jnp.float32),
        jnp.sum(d_gate.astype(jnp.float32), axis=0),
        jnp.dot(joined_reset.T, d_cand, preferred_element_type=jnp.float32),
        jnp.sum(d_cand.astype(jnp.float32), axis=0),
    )
    return (new_state, d_mixed, d_second, grad_sums)


def relation_mats(adjacency, edge_number):
    neighbour = adjacency[:, edge_number, 0]
    far_edge = adjacency[:, edge_number, 1]
    labels = jnp.arange(adjacency.shape[0], dtype=jnp.int32)
    matches = neighbour[:, None] == labels[None, :]
    opposite = (far_edge == (edge_number + 2) % 4)[:, None]
    mirror_mat = jnp.where(jnp.logical_and(matches, opposite), 1.0, 0.0).astype(jnp.bfloat16)
    turned_mat = jnp.where(jnp.logical_and(matches, jnp.logical_not(opposite)), 1.0, 0.0).astype(
        jnp.bfloat16
    )
    return (mirror_mat, turned_mat)


def pick_lines(relation, edge_lines):
    return jnp.einsum("fg,gpc->fpc", relation, edge_lines, preferred_element_type=jnp.float32)


def return_lines(relation, edge_lines):
    return jnp.einsum(
        "fg,fpc->gpc", relation, edge_lines, preferred_element_type=jnp.float32
    ).astype(jnp.bfloat16)


def face_step(edge_lines, offset):
    return passed_along(edge_lines, "tile", offset)


def across_pole(payload, layout):
    tile_x, tile_y, tiles_side, width_bits, tile_index, relations = layout
    result = payload
    for section_number in range(width_bits):
        arrived = result
        for bit_number in (1 + section_number, 1 + width_bits + section_number):
            arrived = swapped(arrived, "tile", bit_number)
        low_bit = tile_index >> 1 + section_number & 1
        high_bit = tile_index >> 1 + width_bits + section_number & 1
        result = jnp.where(low_bit != high_bit, arrived, result)
    return result


def column_halos(grid_field, layout):
    tile_x, tile_y, tiles_side, width_bits, tile_index, relations = layout
    west_line = grid_field[:, :, 0]
    east_line = grid_field[:, :, -1]
    from_west = face_step(east_line, 2)
    wrap_west = face_step(east_line, -2 * (tiles_side - 1))
    from_east = face_step(west_line, -2)
    wrap_east = face_step(west_line, 2 * (tiles_side - 1))
    turned = across_pole(jnp.stack([grid_field[:, 0], grid_field[:, -1]]), layout)
    west_edge = pick_lines(relations[3][0], wrap_west) + pick_lines(relations[3][1], turned[0])
    east_edge = pick_lines(relations[1][0], wrap_east) + pick_lines(relations[1][1], turned[1])
    west_halo = jnp.where(tile_x > 0, from_west, west_edge.astype(jnp.bfloat16))
    east_halo = jnp.where(tile_x < tiles_side - 1, from_east, east_edge.astype(jnp.bfloat16))
    return (west_halo, east_halo)


def row_halos(grid_field, layout):
    tile_x, tile_y, tiles_side, width_bits, tile_index, relations = layout
    from_north = face_step(grid_field[:, -1], 2 * tiles_side)
    from_south = face_step(grid_field[:, 0], -2 * tiles_side)
    turned = across_pole(jnp.stack([grid_field[:, :, 0], grid_field[:, :, -1]]), layout)
    north_edge = pick_lines(relations[0][0], from_north) + pick_lines(relations[0][1], turned[0])
    south_edge = pick_lines(relations[2][0], from_south) + pick_lines(relations[2][1], turned[1])
    north_halo = jnp.where(tile_y > 0, from_north, north_edge.astype(jnp.bfloat16))
    south_halo = jnp.where(tile_y < tiles_side - 1, from_south, south_edge.astype(jnp.bfloat16))
    return (north_halo, south_halo)


def rows_back(d_second, padded_rows, taps_row, layout):
    tile_x, tile_y, tiles_side, width_bits, tile_index, relations = layout
    extent = d_second.shape[1]
    d_values = d_second.astype(jnp.float32)
    grad_taps = jnp.stack(
        [
            jnp.sum(
                d_values * padded_rows[:, tap_number : tap_number + extent].astype(jnp.float32),
                axis=(0, 1, 2),
            )
            for tap_number in range(3)
        ]
    )
    zero_row = jnp.zeros_like(d_values[:, :1])
    shifted = jnp.concatenate([zero_row, d_values, zero_row], axis=1)
    d_first = (
        taps_row[0] * shifted[:, 2:]
        + taps_row[1] * shifted[:, 1:-1]
        + taps_row[2] * shifted[:, :-2]
    )
    north_cot = d_second[:, 0]
    south_cot = d_second[:, -1]
    zero_line = jnp.zeros_like(north_cot)
    back_north = jnp.where(tile_y > 0, north_cot, return_lines(relations[0][0], north_cot))
    back_south = jnp.where(
        tile_y < tiles_side - 1, south_cot, return_lines(relations[2][0], south_cot)
    )
    to_south_row = face_step(back_north, -2 * tiles_side)
    to_north_row = face_step(back_south, 2 * tiles_side)
    turned = across_pole(
        jnp.stack(
            [
                jnp.where(tile_y == 0, return_lines(relations[0][1], north_cot), zero_line),
                jnp.where(
                    tile_y == tiles_side - 1, return_lines(relations[2][1], south_cot), zero_line
                ),
            ]
        ),
        layout,
    )
    d_first = d_first.at[:, -1].add(taps_row[0] * to_south_row.astype(jnp.float32))
    d_first = d_first.at[:, 0].add(taps_row[2] * to_north_row.astype(jnp.float32))
    d_first = d_first.at[:, :, 0].add(taps_row[0] * turned[0].astype(jnp.float32))
    d_first = d_first.at[:, :, -1].add(taps_row[2] * turned[1].astype(jnp.float32))
    return (d_first, grad_taps)


def columns_back(d_first, padded_cols, taps_row, layout):
    tile_x, tile_y, tiles_side, width_bits, tile_index, relations = layout
    extent = d_first.shape[2]
    d_values = d_first.astype(jnp.float32)
    grad_taps = jnp.stack(
        [
            jnp.sum(
                d_values * padded_cols[:, :, tap_number : tap_number + extent].astype(jnp.float32),
                axis=(0, 1, 2),
            )
            for tap_number in range(3)
        ]
    )
    zero_col = jnp.zeros_like(d_values[:, :, :1])
    shifted = jnp.concatenate([zero_col, d_values, zero_col], axis=2)
    d_field = (
        taps_row[0] * shifted[:, :, 2:]
        + taps_row[1] * shifted[:, :, 1:-1]
        + taps_row[2] * shifted[:, :, :-2]
    )
    west_cot = d_first[:, :, 0]
    east_cot = d_first[:, :, -1]
    zero_line = jnp.zeros_like(west_cot)
    inner_west = jnp.where(tile_x > 0, west_cot, zero_line)
    outer_west = jnp.where(tile_x == 0, return_lines(relations[3][0], west_cot), zero_line)
    inner_east = jnp.where(tile_x < tiles_side - 1, east_cot, zero_line)
    outer_east = jnp.where(
        tile_x == tiles_side - 1, return_lines(relations[1][0], east_cot), zero_line
    )
    east_from_inner = face_step(inner_west, -2)
    east_from_outer = face_step(outer_west, 2 * (tiles_side - 1))
    west_from_inner = face_step(inner_east, 2)
    west_from_outer = face_step(outer_east, -2 * (tiles_side - 1))
    turned = across_pole(
        jnp.stack(
            [
                jnp.where(tile_x == 0, return_lines(relations[3][1], west_cot), zero_line),
                jnp.where(
                    tile_x == tiles_side - 1, return_lines(relations[1][1], east_cot), zero_line
                ),
            ]
        ),
        layout,
    )
    d_field = d_field.at[:, :, -1].add(
        taps_row[0] * (east_from_inner.astype(jnp.float32) + east_from_outer.astype(jnp.float32))
    )
    d_field = d_field.at[:, :, 0].add(
        taps_row[2] * (west_from_inner.astype(jnp.float32) + west_from_outer.astype(jnp.float32))
    )
    d_field = d_field.at[:, 0].add(taps_row[0] * turned[0].astype(jnp.float32))
    d_field = d_field.at[:, -1].add(taps_row[2] * turned[1].astype(jnp.float32))
    return (d_field, grad_taps)


def on_device(
    inputs,
    state,
    cotangent,
    adjacency,
    taps,
    gain,
    w_up,
    b_up,
    w_down,
    b_down,
    w_gates,
    b_gates,
    w_cand,
    b_cand,
):
    grid_field = inputs[0, 0]
    extent = grid_field.shape[1]
    channels = grid_field.shape[3]
    tile_count = lax.axis_size("tile")
    width_bits = (tile_count.bit_length() - 2) // 2
    tiles_side = 2**width_bits
    tile_index = lax.axis_index("tile")
    tile_x = tile_index // 2 % tiles_side
    tile_y = tile_index // 2 // tiles_side
    relations = [relation_mats(adjacency, edge_number) for edge_number in range(4)]
    layout = (tile_x, tile_y, tiles_side, width_bits, tile_index, relations)
    taps_f = taps.astype(jnp.float32)
    west_halo, east_halo = column_halos(grid_field, layout)
    padded_cols = jnp.concatenate(
        [west_halo[:, :, None], grid_field, east_halo[:, :, None]], axis=2
    )
    first_pass = sum(
        (
            taps_f[0, tap_number]
            * padded_cols[:, :, tap_number : tap_number + extent].astype(jnp.float32)
            for tap_number in range(3)
        )
    )
    first_pass = lax.optimization_barrier(first_pass.astype(jnp.bfloat16))
    north_halo, south_halo = row_halos(first_pass, layout)
    padded_rows = jnp.concatenate([north_halo[:, None], first_pass, south_halo[:, None]], axis=1)
    second_pass = sum(
        (
            taps_f[1, tap_number]
            * padded_rows[:, tap_number : tap_number + extent].astype(jnp.float32)
            for tap_number in range(3)
        )
    )
    new_rows, d_mixed, d_second, grad_sums = cell_step(
        grid_field.reshape(-1, channels),
        state[0, 0].reshape(-1, channels),
        cotangent[0, 0].reshape(-1, channels),
        second_pass.reshape(-1, channels),
        gain,
        w_up,
        b_up,
        w_down,
        b_down,
        w_gates,
        b_gates,
        w_cand,
        b_cand,
    )
    d_first, grad_rows = rows_back(
        d_second.reshape(grid_field.shape), padded_rows, taps_f[1], layout
    )
    d_first_round = lax.optimization_barrier(d_first.astype(jnp.bfloat16))
    d_field, grad_cols = columns_back(d_first_round, padded_cols, taps_f[0], layout)
    grad_input = (d_field + d_mixed.reshape(grid_field.shape).astype(jnp.float32)).astype(
        jnp.bfloat16
    )
    grad_taps = jnp.stack([grad_cols, grad_rows])
    gain_sum, up_sum, bup_sum, down_sum, bdown_sum, gates_sum, bgates_sum, cand_sum, bcand_sum = (
        grad_sums
    )
    summed = lax.psum(
        (
            grad_taps,
            gain_sum,
            up_sum,
            bup_sum,
            down_sum,
            bdown_sum,
            gates_sum,
            bgates_sum,
            cand_sum,
            bcand_sum,
        ),
        ("tile", "date"),
    )
    norm_factor = float(
        grid_field.shape[0] * extent * extent * tile_count * lax.axis_size("date")
    ) ** (-0.5)
    finished = tuple(((grad_piece * norm_factor).astype(jnp.bfloat16) for grad_piece in summed))
    return (new_rows.reshape(inputs.shape), grad_input[None, None]) + finished


def solution(mesh):
    placed = (
        P("tile", "date", None, None, None, None),
        P("tile", "date", None, None, None, None),
        P("tile", "date", None, None, None, None),
        P(),
        P(),
        P(),
        P(),
        P(),
        P(),
        P(),
        P(),
        P(),
        P(),
        P(),
    )
    return jax.shard_map(
        on_device,
        mesh=mesh,
        in_specs=placed,
        out_specs=(
            P("tile", "date", None, None, None, None),
            P("tile", "date", None, None, None, None),
            P(),
            P(),
            P(),
            P(),
            P(),
            P(),
            P(),
            P(),
            P(),
            P(),
        ),
        check_vma=False,
    )
```

profile of v0, /device:TPU:1, one launch (start us, length us, event | category | flops | bytes accessed | tf_op | source)
XLA Modules:
  0.0 468.4 jit_solution(18293643416147957473)
XLA Ops:
  8.4 7.7 %collective-permute-start.1 = (bf16[12,8,192]{2,1,0:T(8,128)(2,1)S(1)}, bf16[12,8,192]{2,1,0:T(8,128)(2,1)S(1)}, u32[]{:S(2)}, u32[]{:S(2)}) collective-permute-start(bf16[12,8,192]{2,1,0:T(8,128)(2,1)S(1)} %get-tuple-element.230), channel_id=1, source_target_pairs={{0,456},{4,460},{8,464},{12,468},{16,472},{20,476},{24,480},{28,48... | collective-permute-start | bytes 110600 | tf_op jit(solution)/shard_map/ppermute | solution.py:12
  16.1 4.0 collective-permute-start
  23.7 8.4 %collective-permute-start.8 = (bf16[12,8,192]{2,1,0:T(8,128)(2,1)S(1)}, bf16[12,8,192]{2,1,0:T(8,128)(2,1)S(1)}, u32[]{:S(2)}, u32[]{:S(2)}) collective-permute-start(bf16[12,8,192]{2,1,0:T(8,128)(2,1)S(1)} %get-tuple-element.231), channel_id=1, source_target_pairs={{0,504},{4,508},{8,0},{12,4},{16,8},{20,12},{24,16},{28,20},{32,24... | collective-permute-start | bytes 110600 | tf_op jit(solution)/shard_map/ppermute | solution.py:12
  46.2 4.6 collective-permute-done.4
  53.2 4.6 collective-permute-done.5
  60.5 6.6 %collective-permute-done.6 = bf16[2,12,8,192]{3,2,1,0:T(8,128)(2,1)S(1)} collective-permute-done((bf16[2,12,8,192]{3,2,1,0:T(8,128)(2,1)S(1)}, bf16[2,12,8,192]{3,2,1,0:T(8,128)(2,1)S(1)}, u32[]{:S(2)}, u32[]{:S(2)}) %collective-permute-start.6) | collective-permute-done | bytes 73760 | tf_op jit(solution)/shard_map/ppermute | solution.py:18
  67.1 5.1 %collective-permute-start.7 = (bf16[2,12,8,192]{3,2,1,0:T(8,128)(2,1)S(1)}, bf16[2,12,8,192]{3,2,1,0:T(8,128)(2,1)S(1)}, u32[]{:S(2)}, u32[]{:S(2)}) collective-permute-start(bf16[2,12,8,192]{3,2,1,0:T(8,128)(2,1)S(1)} %collective-permute-done.6), channel_id=1, source_target_pairs={{0,256},{4,260},{8,264},{12,268},{16,272},{20,276},{24,280},{28,28... | collective-permute-start | bytes 221192 | tf_op jit(solution)/shard_map/ppermute | solution.py:18
  72.4 5.0 %collective-permute-done.7 = bf16[2,12,8,192]{3,2,1,0:T(8,128)(2,1)S(1)} collective-permute-done((bf16[2,12,8,192]{3,2,1,0:T(8,128)(2,1)S(1)}, bf16[2,12,8,192]{3,2,1,0:T(8,128)(2,1)S(1)}, u32[]{:S(2)}, u32[]{:S(2)}) %collective-permute-start.7) | collective-permute-done | bytes 73760 | tf_op jit(solution)/shard_map/ppermute | solution.py:18
  101.5 4.6 collective-permute-start.17
  106.1 4.7 %collective-permute-start.15 = (bf16[2,12,8,192]{3,2,1,0:T(8,128)(2,1)S(1)}, bf16[2,12,8,192]{3,2,1,0:T(8,128)(2,1)S(1)}, u32[]{:S(2)}, u32[]{:S(2)}) collective-permute-start(bf16[2,12,8,192]{3,2,1,0:T(8,128)(2,1)S(1)} %broadcast_select_fusion.6), channel_id=1, source_target_pairs={{0,32},{4,36},{8,40},{12,44},{16,48},{20,52},{24,56},{28,60},{32,0... | collective-permute-start | bytes 221192 | tf_op jit(solution)/shard_map/ppermute | solution.py:18
  111.0 4.4 collective-permute-done.15
  115.5 5.2 %collective-permute-start.16 = (bf16[2,12,8,192]{3,2,1,0:T(8,128)(2,1)S(1)}, bf16[2,12,8,192]{3,2,1,0:T(8,128)(2,1)S(1)}, u32[]{:S(2)}, u32[]{:S(2)}) collective-permute-start(bf16[2,12,8,192]{3,2,1,0:T(8,128)(2,1)S(1)} %collective-permute-done.15), channel_id=1, source_target_pairs={{0,256},{4,260},{8,264},{12,268},{16,272},{20,276},{24,280},{28,28... | collective-permute-start | bytes 221192 | tf_op jit(solution)/shard_map/ppermute | solution.py:18
  120.9 4.0 collective-permute-done.16
  161.8 4.0 collective-permute-start.21
  168.1 4.4 collective-permute-start.22
  174.5 4.3 collective-permute-start.23
  180.9 6.9 %collective-permute-start.24 = (bf16[2,12,8,192]{3,2,1,0:T(8,128)(2,1)S(1)}, bf16[2,12,8,192]{3,2,1,0:T(8,128)(2,1)S(1)}, u32[]{:S(2)}, u32[]{:S(2)}) collective-permute-start(bf16[2,12,8,192]{3,2,1,0:T(8,128)(2,1)S(1)} %broadcast_select_fusion.5), channel_id=1, source_target_pairs={{0,32},{4,36},{8,40},{12,44},{16,48},{20,52},{24,56},{28,60},{32,0... | collective-permute-start | bytes 221192 | tf_op jit(solution)/shard_map/ppermute | solution.py:18
  191.7 6.7 %collective-permute-start.25 = (bf16[2,12,8,192]{3,2,1,0:T(8,128)(2,1)S(1)}, bf16[2,12,8,192]{3,2,1,0:T(8,128)(2,1)S(1)}, u32[]{:S(2)}, u32[]{:S(2)}) collective-permute-start(bf16[2,12,8,192]{3,2,1,0:T(8,128)(2,1)S(1)} %collective-permute-done.24), channel_id=1, source_target_pairs={{0,256},{4,260},{8,264},{12,268},{16,272},{20,276},{24,280},{28,28... | collective-permute-start | bytes 221192 | tf_op jit(solution)/shard_map/ppermute | solution.py:18
  198.6 3.9 scatter-add.29
  204.0 120.7 %all-reduce.4 = (f32[2,3,192]{2,1,0:T(4,128)S(1)}, f32[192]{0:T(256)S(1)}, f32[768]{0:T(1024)S(1)}, f32[192]{0:T(256)S(1)}, f32[384]{0:T(512)S(1)}, /*index=5*/f32[192]{0:T(256)S(1)}) all-reduce(f32[2,3,192]{2,1,0:T(4,128)S(1)} %pad_maximum_fusion.17, f32[192]{0:T(256)S(1)} %copy-done.59, ...), channel_id=1, replica_groups=mesh['tile'=128,'date'=4] {'tile','date'}, use_global_device_ids=true, to_apply=%region_10.11 | all-reduce | flops 2880 | bytes 23040 | tf_op jit(solution)/shard_map/psum | solution.py:354
  336.2 4.1 collective-permute-start.26
  355.5 4.5 collective-permute-start.34
  370.2 4.0 collective-permute-done.35
  375.1 81.3 %all-reduce.8.cloned.1.call-done = (f32[192,768]{1,0:T(8,128)}, f32[768,192]{0,1:T(8,128)}, f32[384,384]{1,0:T(8,128)}, f32[384,192]{0,1:T(8,128)}) async-done(((f32[192,768]{1,0:T(8,128)}, f32[768,192]{0,1:T(8,128)}, f32[384,384]{1,0:T(8,128)}, f32[384,192]{0,1:T(8,128)}), (f32[192,768]{1,0:T(8,128)}, f32[768,192]{0,1:T(8,128)}, f32[384,384]{1,0:T(8,128)}, ...) | async-done | bytes 2064400 | tf_op jit(solution)/shard_map/psum | solution.py:354
  (324 shorter events, 138.9 us)
Async XLA Ops:
  7.2 449.1 %all-reduce.8.cloned.1.call-start = ((), (), s32[]{:S(2)}) async-start(), calls=%async_computation | async-start | bytes 4128768 | tf_op jit(solution)/shard_map/psum | solution.py:354
  8.4 51.9 %collective-permute-start.1 = (bf16[12,8,192]{2,1,0:T(8,128)(2,1)S(1)}, bf16[12,8,192]{2,1,0:T(8,128)(2,1)S(1)}, u32[]{:S(2)}, u32[]{:S(2)}) collective-permute-start(bf16[12,8,192]{2,1,0:T(8,128)(2,1)S(1)} %get-tuple-element.230), channel_id=1, source_target_pairs={{0,456},{4,460},{8,464},{12,468},{16,472},{20,476},{24,480},{28,48... | collective-permute-start | bytes 110600 | tf_op jit(solution)/shard_map/ppermute | solution.py:12
  16.1 61.5 %collective-permute-start = (bf16[12,8,192]{2,1,0:T(8,128)(2,1)S(1)}, bf16[12,8,192]{2,1,0:T(8,128)(2,1)S(1)}, u32[]{:S(2)}, u32[]{:S(2)}) collective-permute-start(bf16[12,8,192]{2,1,0:T(8,128)(2,1)S(1)} %get-tuple-element.230), channel_id=1, source_target_pairs={{0,8},{4,12},{8,16},{12,20},{16,24},{20,28},{24,32},{28,36},{32,40... | collective-permute-start | bytes 110600 | tf_op jit(solution)/shard_map/ppermute | solution.py:12
  20.1 52.1 %collective-permute-start.9 = (bf16[12,8,192]{2,1,0:T(8,128)(2,1)S(1)}, bf16[12,8,192]{2,1,0:T(8,128)(2,1)S(1)}, u32[]{:S(2)}, u32[]{:S(2)}) collective-permute-start(bf16[12,8,192]{2,1,0:T(8,128)(2,1)S(1)} %get-tuple-element.231), channel_id=1, source_target_pairs={{0,56},{4,60},{8,64},{12,68},{16,72},{20,76},{24,80},{28,84},{32,8... | collective-permute-start | bytes 110600 | tf_op jit(solution)/shard_map/ppermute | solution.py:12
  23.7 54.3 %collective-permute-start.8 = (bf16[12,8,192]{2,1,0:T(8,128)(2,1)S(1)}, bf16[12,8,192]{2,1,0:T(8,128)(2,1)S(1)}, u32[]{:S(2)}, u32[]{:S(2)}) collective-permute-start(bf16[12,8,192]{2,1,0:T(8,128)(2,1)S(1)} %get-tuple-element.231), channel_id=1, source_target_pairs={{0,504},{4,508},{8,0},{12,4},{16,8},{20,12},{24,16},{28,20},{32,24... | collective-permute-start | bytes 110600 | tf_op jit(solution)/shard_map/ppermute | solution.py:12
  57.8 9.3 %collective-permute-start.6 = (bf16[2,12,8,192]{3,2,1,0:T(8,128)(2,1)S(1)}, bf16[2,12,8,192]{3,2,1,0:T(8,128)(2,1)S(1)}, u32[]{:S(2)}, u32[]{:S(2)}) collective-permute-start(bf16[2,12,8,192]{3,2,1,0:T(8,128)(2,1)S(1)} %broadcast_select_fusion.7), channel_id=1, source_target_pairs={{0,32},{4,36},{8,40},{12,44},{16,48},{20,52},{24,56},{28,60},{32,0... | collective-permute-start | bytes 221192 | tf_op jit(solution)/shard_map/ppermute | solution.py:18
  67.1 10.3 %collective-permute-start.7 = (bf16[2,12,8,192]{3,2,1,0:T(8,128)(2,1)S(1)}, bf16[2,12,8,192]{3,2,1,0:T(8,128)(2,1)S(1)}, u32[]{:S(2)}, u32[]{:S(2)}) collective-permute-start(bf16[2,12,8,192]{3,2,1,0:T(8,128)(2,1)S(1)} %collective-permute-done.6), channel_id=1, source_target_pairs={{0,256},{4,260},{8,264},{12,268},{16,272},{20,276},{24,280},{28,28... | collective-permute-start | bytes 221192 | tf_op jit(solution)/shard_map/ppermute | solution.py:18
  97.5 8.6 %collective-permute-start.14 = (bf16[2,12,8,192]{3,2,1,0:T(8,128)(2,1)}, bf16[2,12,8,192]{3,2,1,0:T(8,128)(2,1)S(1)}, u32[]{:S(2)}, u32[]{:S(2)}) collective-permute-start(bf16[2,12,8,192]{3,2,1,0:T(8,128)(2,1)} %collective-permute-done.13), channel_id=1, source_target_pairs={{0,128},{4,132},{8,136},{12,140},{16,144},{20,148},{24,152},{28,15... | collective-permute-start | bytes 221192 | tf_op jit(solution)/shard_map/ppermute | solution.py:18
  99.5 11.3 %collective-permute-start.10 = (bf16[12,8,192]{2,0,1:T(8,128)(2,1)S(1)}, bf16[12,8,192]{2,0,1:T(8,128)(2,1)S(1)}, u32[]{:S(2)}, u32[]{:S(2)}) collective-permute-start(bf16[12,8,192]{2,0,1:T(8,128)(2,1)S(1)} %bitcast.239), channel_id=1, source_target_pairs={{0,64},{4,68},{8,72},{12,76},{16,80},{20,84},{24,88},{28,92},{32,9... | collective-permute-start | bytes 110600 | tf_op jit(solution)/shard_map/ppermute | solution.py:12
  101.5 19.2 %collective-permute-start.17 = (bf16[12,8,192]{2,0,1:T(8,128)(2,1)S(1)}, bf16[12,8,192]{2,0,1:T(8,128)(2,1)S(1)}, u32[]{:S(2)}, u32[]{:S(2)}) collective-permute-start(bf16[12,8,192]{2,0,1:T(8,128)(2,1)S(1)} %bitcast.238), channel_id=1, source_target_pairs={{0,448},{4,452},{8,456},{12,460},{16,464},{20,468},{24,472},{28,47... | collective-permute-start | bytes 110600 | tf_op jit(solution)/shard_map/ppermute | solution.py:12
  106.1 9.4 %collective-permute-start.15 = (bf16[2,12,8,192]{3,2,1,0:T(8,128)(2,1)S(1)}, bf16[2,12,8,192]{3,2,1,0:T(8,128)(2,1)S(1)}, u32[]{:S(2)}, u32[]{:S(2)}) collective-permute-start(bf16[2,12,8,192]{3,2,1,0:T(8,128)(2,1)S(1)} %broadcast_select_fusion.6), channel_id=1, source_target_pairs={{0,32},{4,36},{8,40},{12,44},{16,48},{20,52},{24,56},{28,60},{32,0... | collective-permute-start | bytes 221192 | tf_op jit(solution)/shard_map/ppermute | solution.py:18
  115.5 9.4 %collective-permute-start.16 = (bf16[2,12,8,192]{3,2,1,0:T(8,128)(2,1)S(1)}, bf16[2,12,8,192]{3,2,1,0:T(8,128)(2,1)S(1)}, u32[]{:S(2)}, u32[]{:S(2)}) collective-permute-start(bf16[2,12,8,192]{3,2,1,0:T(8,128)(2,1)S(1)} %collective-permute-done.15), channel_id=1, source_target_pairs={{0,256},{4,260},{8,264},{12,268},{16,272},{20,276},{24,280},{28,28... | collective-permute-start | bytes 221192 | tf_op jit(solution)/shard_map/ppermute | solution.py:18
  150.7 11.1 %collective-permute-start.20 = (bf16[2,12,8,192]{3,2,1,0:T(8,128)(2,1)}, bf16[2,12,8,192]{3,2,1,0:T(8,128)(2,1)}, u32[]{:S(2)}, u32[]{:S(2)}) collective-permute-start(bf16[2,12,8,192]{3,2,1,0:T(8,128)(2,1)} %pad_maximum_fusion.15), channel_id=1, source_target_pairs={{0,8},{4,12},{8,0},{12,4},{16,24},{20,28},{24,16},{28,20},{32,40},... | collective-permute-start | bytes 221192 | tf_op jit(solution)/shard_map/ppermute | solution.py:18
  152.7 19.8 %collective-permute-start.18 = (bf16[12,8,192]{2,0,1:T(8,128)(2,1)}, bf16[12,8,192]{2,0,1:T(8,128)(2,1)}, u32[]{:S(2)}, u32[]{:S(2)}) collective-permute-start(bf16[12,8,192]{2,0,1:T(8,128)(2,1)} %fusion.12), channel_id=1, source_target_pairs={{0,448},{4,452},{8,456},{12,460},{16,464},{20,468},{24,472},{28,47... | collective-permute-start | bytes 110600 | tf_op jit(solution)/shard_map/ppermute | solution.py:12
  157.9 29.9 %collective-permute-start.19 = (bf16[12,8,192]{2,0,1:T(8,128)(2,1)S(1)}, bf16[12,8,192]{2,0,1:T(8,128)(2,1)S(1)}, u32[]{:S(2)}, u32[]{:S(2)}) collective-permute-start(bf16[12,8,192]{2,0,1:T(8,128)(2,1)S(1)} %copy-done.60), channel_id=1, source_target_pairs={{0,64},{4,68},{8,72},{12,76},{16,80},{20,84},{24,88},{28,92},{32,9... | collective-permute-start | bytes 110600 | tf_op jit(solution)/shard_map/ppermute | solution.py:12
  180.9 10.8 %collective-permute-start.24 = (bf16[2,12,8,192]{3,2,1,0:T(8,128)(2,1)S(1)}, bf16[2,12,8,192]{3,2,1,0:T(8,128)(2,1)S(1)}, u32[]{:S(2)}, u32[]{:S(2)}) collective-permute-start(bf16[2,12,8,192]{3,2,1,0:T(8,128)(2,1)S(1)} %broadcast_select_fusion.5), channel_id=1, source_target_pairs={{0,32},{4,36},{8,40},{12,44},{16,48},{20,52},{24,56},{28,60},{32,0... | collective-permute-start | bytes 221192 | tf_op jit(solution)/shard_map/ppermute | solution.py:18
  191.7 10.8 %collective-permute-start.25 = (bf16[2,12,8,192]{3,2,1,0:T(8,128)(2,1)S(1)}, bf16[2,12,8,192]{3,2,1,0:T(8,128)(2,1)S(1)}, u32[]{:S(2)}, u32[]{:S(2)}) collective-permute-start(bf16[2,12,8,192]{3,2,1,0:T(8,128)(2,1)S(1)} %collective-permute-done.24), channel_id=1, source_target_pairs={{0,256},{4,260},{8,264},{12,268},{16,272},{20,276},{24,280},{28,28... | collective-permute-start | bytes 221192 | tf_op jit(solution)/shard_map/ppermute | solution.py:18
  331.9 8.4 %collective-permute-start.31 = (bf16[2,12,8,192]{3,2,1,0:T(8,128)(2,1)S(1)}, bf16[2,12,8,192]{3,2,1,0:T(8,128)(2,1)S(1)}, u32[]{:S(2)}, u32[]{:S(2)}) collective-permute-start(bf16[2,12,8,192]{3,2,1,0:T(8,128)(2,1)S(1)} %collective-permute-done.30), channel_id=1, source_target_pairs={{0,64},{4,68},{8,72},{12,76},{16,80},{20,84},{24,88},{28,92},{32,9... | collective-permute-start | bytes 221192 | tf_op jit(solution)/shard_map/ppermute | solution.py:18
  336.2 23.8 %collective-permute-start.26 = (bf16[12,8,192]{2,1,0:T(8,128)(2,1)S(1)}, bf16[12,8,192]{2,1,0:T(8,128)(2,1)S(1)}, u32[]{:S(2)}, u32[]{:S(2)}) collective-permute-start(bf16[12,8,192]{2,1,0:T(8,128)(2,1)S(1)} %get-tuple-element.221), channel_id=1, source_target_pairs={{0,504},{4,508},{8,0},{12,4},{16,8},{20,12},{24,16},{28,20},{32,24... | collective-permute-start | bytes 110600 | tf_op jit(solution)/shard_map/ppermute | solution.py:12
  342.3 17.7 %collective-permute-start.27 = (bf16[12,8,192]{2,1,0:T(8,128)(2,1)S(1)}, bf16[12,8,192]{2,1,0:T(8,128)(2,1)S(1)}, u32[]{:S(2)}, u32[]{:S(2)}) collective-permute-start(bf16[12,8,192]{2,1,0:T(8,128)(2,1)S(1)} %fusion.91), channel_id=1, source_target_pairs={{0,56},{4,60},{8,64},{12,68},{16,72},{20,76},{24,80},{28,84},{32,8... | collective-permute-start | bytes 110600 | tf_op jit(solution)/shard_map/ppermute | solution.py:12
  345.0 23.7 %collective-permute-start.28 = (bf16[12,8,192]{2,1,0:T(8,128)(2,1)S(1)}, bf16[12,8,192]{2,1,0:T(8,128)(2,1)S(1)}, u32[]{:S(2)}, u32[]{:S(2)}) collective-permute-start(bf16[12,8,192]{2,1,0:T(8,128)(2,1)S(1)} %get-tuple-element.220), channel_id=1, source_target_pairs={{0,8},{4,12},{8,16},{12,20},{16,24},{20,28},{24,32},{28,36},{32,40... | collective-permute-start | bytes 110600 | tf_op jit(solution)/shard_map/ppermute | solution.py:12
  350.8 18.0 %collective-permute-start.29 = (bf16[12,8,192]{2,1,0:T(8,128)(2,1)S(1)}, bf16[12,8,192]{2,1,0:T(8,128)(2,1)S(1)}, u32[]{:S(2)}, u32[]{:S(2)}) collective-permute-start(bf16[12,8,192]{2,1,0:T(8,128)(2,1)S(1)} %fusion.92), channel_id=1, source_target_pairs={{0,456},{4,460},{8,464},{12,468},{16,472},{20,476},{24,480},{28,48... | collective-permute-start | bytes 110600 | tf_op jit(solution)/shard_map/ppermute | solution.py:12
  355.5 9.3 %collective-permute-start.34 = (bf16[2,12,8,192]{3,2,1,0:T(8,128)(2,1)S(1)}, bf16[2,12,8,192]{3,2,1,0:T(8,128)(2,1)S(1)}, u32[]{:S(2)}, u32[]{:S(2)}) collective-permute-start(bf16[2,12,8,192]{3,2,1,0:T(8,128)(2,1)S(1)} %broadcast_select_fusion.4), channel_id=1, source_target_pairs={{0,32},{4,36},{8,40},{12,44},{16,48},{20,52},{24,56},{28,60},{32,0... | collective-permute-start | bytes 221192 | tf_op jit(solution)/shard_map/ppermute | solution.py:18
  364.9 9.3 %collective-permute-start.35 = (bf16[2,12,8,192]{3,2,1,0:T(8,128)(2,1)S(1)}, bf16[2,12,8,192]{3,2,1,0:T(8,128)(2,1)S(1)}, u32[]{:S(2)}, u32[]{:S(2)}) collective-permute-start(bf16[2,12,8,192]{3,2,1,0:T(8,128)(2,1)S(1)} %collective-permute-done.34), channel_id=1, source_target_pairs={{0,256},{4,260},{8,264},{12,268},{16,272},{20,276},{24,280},{28,28... | collective-permute-start | bytes 221192 | tf_op jit(solution)/shard_map/ppermute | solution.py:18
  (77 other events, 935.7 us)
Sparse Core Ops, SparseCore 0:
  161.8 294.5 all-reduce.7
where the time goes:
time: 470 us; the launch traced here: 468 us
  waiting for transfers between devices  135 us (29%)
  starting transfers between devices  130 us (28%)
  blocking collectives  121 us (26%)
  local copies, waits for them, and re-layouts  24.4 us (5%)
  other arithmetic  23 us (5%)
  matrix products  19.1 us (4%)
  between operations  15.9 us (3%)
    psum x1, blocking collectives, on_device(): lax.psum((grad_taps, gain_sum, up_sum, bup_sum, down_sum, bdown_sum, gate...  121 us
    psum x1, waiting for transfers between devices, on_device(): lax.psum((grad_taps, gain_sum, up_sum, bup_sum, down_sum, bdown_sum, gate...  81.3 us
    ppermute x24, starting transfers between devices, swapped(): return lax.ppermute(value, axis, pairs)  80.7 us
    ppermute x24, waiting for transfers between devices, swapped(): return lax.ppermute(value, axis, pairs)  53.8 us
    ppermute x12, starting transfers between devices, passed_along(): return lax.ppermute(value, axis, pairs)  49.5 us
  transfers between devices with their start and end apart: 37, of which 19 were waited for; matrix products, arithmetic and copies ran while one was open for 7% of the time, Pallas kernels for 0%

commit v1 on v0

v1 whole, which is shorter than its diff:
```python
import functools
import math

import jax
import jax.numpy as jnp
from jax import lax
from jax.experimental import pallas as pl
from jax.experimental.pallas import tpu as pltpu
from jax.sharding import PartitionSpec as P

EPSILON = 1e-06
MESH = pl.DeviceIdType.MESH
F32 = jnp.float32
BF16 = jnp.bfloat16
FACES = 12
SIDE = 8
HALF = 128
X_PART, Y_PART, Z_PART = 64, 32, 32
FIRST_ROW, LAST_ROW, FIRST_COL, LAST_COL = range(4)
GELU_A = math.sqrt(2.0 / math.pi)
GELU_B = 0.044715
ROW_BUP, ROW_BGATES, ROW_TAPS, ROW_GAIN, ROW_BDOWN, ROW_BCAND = 0, 1, 2, 8, 9, 10
SMALL_ROWS = ((0, 6), (1, 3)) + tuple((row, 2) for row in range(2, 11))
CAND_AT, GATES_AT, DOWN_AT, UP_AT, SMALL_AT = 0, 36, 108, 180, 252


def nn(left, right):
    return jnp.dot(left, right, preferred_element_type=F32)


def nt(left, right):
    return lax.dot_general(left, right, (((1,), (1,)), ((), ())), preferred_element_type=F32)


def tn(left, right):
    return lax.dot_general(left, right, (((0,), (0,)), ((), ())), preferred_element_type=F32)


def sigmoid(value):
    return 0.5 + 0.5 * jnp.tanh(0.5 * value)


def store_tiles(slab, at, matrix):
    rows, columns = matrix.shape
    packed = matrix.astype(BF16)
    across = columns // 128
    for row in range(rows // 16):
        for column in range(across):
            slab[at + row * across + column] = packed[
                row * 16 : row * 16 + 16, column * 128 : column * 128 + 128
            ]


def level_kernel(
    side,
    x_low,
    norm_factor,
    adj,
    x_ref,
    h_ref,
    g_ref,
    par,
    w_up,
    w_down_t,
    w_gates,
    w_cand_t,
    ns_out,
    gi_out,
    slab_out,
    snd,
    rcv,
    pool,
    halo,
    field,
    second,
    wg_u,
    wg_r,
    wc_m,
    wc_r,
    normed_s,
    hid_s,
    d_pre_s,
    d_mix_s,
    d_gate_s,
    joined_s,
    d_cand_s,
    d_sec_s,
    small,
    tile32,
    slab,
    core_rcv,
    t1,
    x_rcv,
    y_rcv,
    z_rcv,
    t2,
    b0_rcv,
    b1_rcv,
    b2_rcv,
    b3_rcv,
    cz,
    cy,
    gathered,
    halo_send,
    halo_recv,
    red_send,
    red_recv,
):
    channels = x_ref.shape[1]
    nx = 2 * x_low
    unit = 32 // (nx * side)
    tile = lax.axis_index("tile")
    date = lax.axis_index("date")
    ty, tx = tile // 2 // side, tile // 2 % side
    core = date % 2
    mx = (tile % 2) * x_low + date // 2

    def device(x, y, z, c):
        return ((y * side + z) * 2 + x // x_low, (x % x_low) * 2 + c)

    def along(axis, steps):
        if axis == "x":
            return device((mx + steps) % nx, ty, tx, core)
        if axis == "y":
            return device(mx, (ty + steps) % side, tx, core)
        return device(mx, ty, (tx + steps) % side, core)

    sibling = device(mx, ty, tx, 1 - core)
    across = device(mx, tx, ty, core)
    top, bottom = ty == 0, ty == side - 1
    west, east = tx == 0, tx == side - 1
    has_across = jnp.logical_and(
        ty != tx,
        jnp.logical_or(jnp.logical_or(top, bottom), jnp.logical_or(west, east)),
    )

    barrier = pltpu.get_barrier_semaphore()
    peers = [sibling]
    peers += [along("x", step) for step in range(1, nx)]
    peers += [along("y", step) for step in range(1, side)]
    peers += [along("z", step) for step in range(1, side)]
    for peer in peers:
        pl.semaphore_signal(barrier, inc=1, device_id=peer, device_id_type=MESH)

    @pl.when(has_across)
    def _():
        pl.semaphore_signal(barrier, inc=1, device_id=across, device_id_type=MESH)

    pool[...] = jnp.zeros_like(pool)
    small[...] = jnp.zeros_like(small)
    slab[SMALL_AT + 2] = jnp.zeros((16, 128), BF16)
    slab[SMALL_AT + 3] = jnp.zeros((16, 128), BF16)
    wg_u[...] = w_gates[:, :channels]
    wg_r[...] = w_gates[:, channels:]
    wc_m[...] = w_cand_t[:, :channels]
    wc_r[...] = w_cand_t[:, channels:]

    def tap(axis, number):
        row = ROW_TAPS + 3 * axis + number
        return par[row : row + 1, :channels].reshape(1, 1, channels)

    def block(ref, b):
        rows = pl.ds(pl.multiple_of(b * 128, 128), 128)
        return ref[rows, :].astype(F32).reshape(16, 8, channels)

    def put_lines(exchange, b, value, kinds):
        rows = pl.ds(pl.multiple_of(b * 16, 16), 16)
        faces = value.reshape(2, 8, 8, channels)
        for kind in kinds:
            if kind == FIRST_ROW:
                line = faces[:, 0].reshape(16, channels)
            elif kind == LAST_ROW:
                line = faces[:, 7].reshape(16, channels)
            elif kind == FIRST_COL:
                line = value[:, 0, :]
            else:
                line = value[:, 7, :]
            snd[exchange, kind, rows, :] = line.astype(BF16)

    def x_lines(b, carry):
        put_lines(0, b, block(x_ref, b), range(4))
        return carry

    lax.fori_loop(0, 6, x_lines, 0)

    @pl.when(has_across)
    def _():
        pl.semaphore_wait(barrier, len(peers) + 1)

    @pl.when(jnp.logical_not(has_across))
    def _():
        pl.semaphore_wait(barrier, len(peers))

    def halo_copies(exchange):
        on_columns = exchange in (0, 3)
        rows_turn = exchange in (0, 2)
        axis = "z" if on_columns else "y"
        last, first = (LAST_COL, FIRST_COL) if on_columns else (LAST_ROW, FIRST_ROW)
        t_first, t_last = (FIRST_ROW, LAST_ROW) if rows_turn else (FIRST_COL, LAST_COL)
        row_first = jnp.logical_and(top, jnp.logical_not(west))
        row_last = jnp.logical_and(bottom, jnp.logical_not(east))
        col_first = jnp.logical_and(west, jnp.logical_not(top))
        col_last = jnp.logical_and(east, jnp.logical_not(bottom))
        if rows_turn:
            sends, receives = (row_first, row_last), (col_first, col_last)
        else:
            sends, receives = (col_first, col_last), (row_first, row_last)
        targets = (along(axis, 1), along(axis, -1), across, across)
        return [
            (
                pltpu.make_async_remote_copy(
                    src_ref=snd.at[exchange, line],
                    dst_ref=rcv.at[exchange, kind],
                    send_sem=halo_send.at[exchange, kind],
                    recv_sem=halo_recv.at[exchange, kind],
                    device_id=target,
                    device_id_type=MESH,
                ),
                None if kind < 2 else sends[kind - 2],
                None if kind < 2 else receives[kind - 2],
                line,
            )
            for kind, (line, target) in enumerate(zip((last, first, t_first, t_last), targets))
        ]

    def start_halos(exchange):
        for copy, sends, _, _ in halo_copies(exchange):
            if sends is None:
                copy.start()
            else:
                pl.when(sends)(copy.start)

    def finish_halo_sends(exchange):
        for copy, sends, _, _ in halo_copies(exchange):
            if sends is None:
                copy.wait_send()
            else:
                pl.when(sends)(copy.wait_send)

    def receive_halos(exchange):
        copies = halo_copies(exchange)
        corners = (jnp.logical_and(top, west), jnp.logical_and(bottom, east))

        def spread(ref, at):
            pool[at[0], at[1] : at[1] + 12] = (
                ref[...].astype(F32).reshape(FACES, SIDE, channels)
            )

        for kind, (copy, _, receives, line) in enumerate(copies):
            if kind < 2:
                copy.wait_recv()
                spread(rcv.at[exchange, kind], (kind, 0))
            else:

                @pl.when(receives)
                def _():
                    copy.wait_recv()
                    spread(rcv.at[exchange, kind], (kind - 2, 12))

                @pl.when(corners[kind - 2])
                def _():
                    spread(snd.at[exchange, line], (kind - 2, 12))

    def beside(face, edge):
        return adj[(face * 4 + edge) * 2], adj[(face * 4 + edge) * 2 + 1] != (edge + 2) % 4

    def gather(to, which, edge, on_border, mode):
        def one(face, carry):
            neighbour, turned = beside(face, edge)
            if mode == "both":
                there = jnp.where(turned, 12 + neighbour, neighbour)
                index = jnp.where(on_border, there, face)
            elif mode == "straight":
                index = jnp.where(on_border, jnp.where(turned, 24, neighbour), face)
            else:
                index = jnp.where(jnp.logical_and(on_border, turned), 12 + neighbour, 24)
            halo[to, face] = pool[which, index]
            return carry

        lax.fori_loop(0, FACES, one, 0)

    def halo_lines(which, b):
        return halo[which, pl.ds(2 * b, 2)]

    place = lax.broadcasted_iota(jnp.int32, (16, 8, channels), 1)

    def upright(lines):
        return jnp.broadcast_to(lines.reshape(16, 1, channels), (16, 8, channels))

    def column_shifts(value, lines_west, lines_east):
        left = jnp.where(place == 0, upright(lines_west), pltpu.roll(value, 1, 1))
        right = jnp.where(place == 7, upright(lines_east), pltpu.roll(value, 7, 1))
        return left, right

    def row_shifts(value, lines_north, lines_south):
        faces = value.reshape(2, 8, 8, channels)
        up = jnp.concatenate([lines_north[:, None], faces[:, :7]], axis=1)
        down = jnp.concatenate([faces[:, 1:], lines_south[:, None]], axis=1)
        return up.reshape(16, 8, channels), down.reshape(16, 8, channels)

    def rounded(value):
        return value.astype(BF16).astype(F32)

    def put_block(ref, b, value):
        rows = pl.ds(pl.multiple_of(b * 128, 128), 128)
        ref[rows, :] = value.reshape(128, channels).astype(ref.dtype)

    start_halos(0)
    receive_halos(0)
    gather(0, 0, 3, west, "both")
    gather(1, 1, 1, east, "both")

    def first_pass(b, carry):
        value = block(x_ref, b)
        left, right = column_shifts(value, halo_lines(0, b), halo_lines(1, b))
        first = rounded(tap(0, 0) * left + tap(0, 1) * value + tap(0, 2) * right)
        put_block(field, b, first)
        put_lines(1, b, first, range(4))
        return carry

    lax.fori_loop(0, 6, first_pass, 0)

    start_halos(1)
    receive_halos(1)
    gather(2, 0, 0, top, "both")
    gather(3, 1, 2, bottom, "both")

    def second_pass(b, carry):
        value = block(field, b)
        up, down = row_shifts(value, halo_lines(2, b), halo_lines(3, b))
        put_block(second, b, tap(1, 0) * up + tap(1, 1) * value + tap(1, 2) * down)
        return carry

    lax.fori_loop(0, 6, second_pass, 0)

    def vector(row, start, size):
        return par[row : row + 1, start : start + size]

    def cell(b, sums):
        rows = pl.ds(pl.multiple_of(b * 256, 256), 256)
        gain = vector(ROW_GAIN, 0, channels)
        centred = second[rows, :]
        centred = centred - jnp.mean(centred, axis=-1, keepdims=True)
        inv_scale = lax.rsqrt(jnp.mean(centred * centred, axis=-1, keepdims=True) + EPSILON)
        standard = centred * inv_scale
        normed = (standard * gain).astype(BF16)
        normed_s[rows, :] = normed
        pre = nn(normed, w_up[...]) + vector(ROW_BUP, 0, w_up.shape[1])
        square = pre * pre
        curve = jnp.tanh(GELU_A * pre * (1.0 + GELU_B * square))
        hid = (0.5 * pre * (1.0 + curve)).astype(BF16)
        hid_s[rows, :] = hid
        slope = 0.5 * (1.0 + curve) + (0.5 * GELU_A) * pre * (1.0 - curve * curve) * (
            1.0 + 3.0 * GELU_B * square
        )
        mixed = (
            x_ref[rows, :].astype(F32)
            + nt(hid, w_down_t[...])
            + vector(ROW_BDOWN, 0, channels)
        ).astype(BF16)
        joined_s[rows, :channels] = mixed
        prior_b = h_ref[rows, :]
        prior = prior_b.astype(F32)
        update = sigmoid(
            nn(mixed, wg_u[:channels])
            + nn(prior_b, wg_u[channels:])
            + vector(ROW_BGATES, 0, channels)
        )
        reset = sigmoid(
            nn(mixed, wg_r[:channels])
            + nn(prior_b, wg_r[channels:])
            + vector(ROW_BGATES, channels, channels)
        )
        reset_state = (reset * prior).astype(BF16)
        joined_s[rows, channels:] = reset_state
        candidate = jnp.tanh(
            nt(mixed, wc_m[...])
            + nt(reset_state, wc_r[...])
            + vector(ROW_BCAND, 0, channels)
        )
        ns_out[rows, :] = ((1.0 - update) * candidate + update * prior).astype(BF16)
        upstream = g_ref[rows, :].astype(F32)
        kept = upstream * (1.0 - update)
        d_cand = (kept * (1.0 - candidate * candidate)).astype(BF16)
        d_cand_s[rows, :] = d_cand
        d_update = (kept * (prior - candidate) * update).astype(BF16)
        d_reset = (nn(d_cand, wc_r[...]) * prior * reset * (1.0 - reset)).astype(BF16)
        d_gate_s[rows, :channels] = d_update
        d_gate_s[rows, channels:] = d_reset
        d_mixed = (
            nn(d_cand, wc_m[...])
            + nt(d_update, wg_u[:channels])
            + nt(d_reset, wg_r[:channels])
        ).astype(BF16)
        d_mix_s[rows, :] = d_mixed
        d_pre = (nn(d_mixed, w_down_t[...]) * slope).astype(BF16)
        d_pre_s[rows, :] = d_pre
        d_normed = nt(d_pre, w_up[...])
        d_standard = d_normed * gain
        d_second = inv_scale * (
            d_standard
            - jnp.mean(d_standard, axis=-1, keepdims=True)
            - standard * jnp.mean(d_standard * standard, axis=-1, keepdims=True)
        )
        d_sec_s[rows, :] = d_second.astype(BF16)

        def total(value):
            return jnp.sum(value.astype(F32), axis=0, keepdims=True)

        extras = (
            total(d_pre),
            total(d_update),
            total(d_reset),
            total(d_normed * standard),
            total(d_mixed),
            total(d_cand),
        )
        return tuple(old + new for old, new in zip(sums, extras))

    zeros = jnp.zeros((1, channels), F32)
    sums = lax.fori_loop(
        0,
        3,
        cell,
        (jnp.zeros((1, w_up.shape[1]), F32), zeros, zeros, zeros, zeros, zeros),
    )
    small[ROW_BUP : ROW_BUP + 1, :] = sums[0]
    small[ROW_BGATES : ROW_BGATES + 1, :channels] = sums[1]
    small[ROW_BGATES : ROW_BGATES + 1, channels : 2 * channels] = sums[2]
    small[ROW_GAIN : ROW_GAIN + 1, :channels] = sums[3]
    small[ROW_BDOWN : ROW_BDOWN + 1, :channels] = sums[4]
    small[ROW_BCAND : ROW_BCAND + 1, :channels] = sums[5]

    def second_lines(b, carry):
        put_lines(2, b, block(d_sec_s, b), (FIRST_ROW, LAST_ROW))
        return carry

    lax.fori_loop(0, 6, second_lines, 0)
    start_halos(2)

    store_tiles(slab, CAND_AT, tn(d_cand_s[...], joined_s[...]))
    store_tiles(slab, GATES_AT, tn(joined_s[:, :channels], d_gate_s[...]))
    store_tiles(slab, GATES_AT + 36, tn(h_ref[...], d_gate_s[...]))
    store_tiles(slab, DOWN_AT, tn(d_mix_s[...], hid_s[...]))
    store_tiles(slab, UP_AT, tn(normed_s[...], d_pre_s[...]))

    regions = ((0, X_PART), (X_PART, Y_PART), (X_PART + Y_PART, Z_PART))

    def remote(src, dst, stage, target):
        return pltpu.make_async_remote_copy(
            src_ref=src,
            dst_ref=dst,
            send_sem=red_send.at[stage],
            recv_sem=red_recv.at[stage],
            device_id=target,
            device_id_type=MESH,
        )

    def core_copy(number):
        at, size = regions[number]
        return remote(
            slab.at[pl.ds((1 - core) * HALF + at, size)],
            core_rcv.at[pl.ds(at, size)],
            number,
            sibling,
        )

    core_copy(0).start()
    core_copy(1).start()

    receive_halos(2)
    gather(4, 0, 0, top, "straight")
    gather(5, 1, 2, bottom, "straight")
    gather(6, 0, 3, west, "turned")
    gather(7, 1, 1, east, "turned")

    def first_back(b, sums):
        value = block(d_sec_s, b)
        up, down = row_shifts(value, halo_lines(4, b), halo_lines(5, b))
        d_first = tap(1, 0) * down + tap(1, 1) * value + tap(1, 2) * up
        d_first += jnp.where(place == 0, tap(1, 0) * upright(halo_lines(6, b)), 0.0)
        d_first += jnp.where(place == 7, tap(1, 2) * upright(halo_lines(7, b)), 0.0)
        first = block(field, b)
        above, below = row_shifts(first, halo_lines(2, b), halo_lines(3, b))
        d_first = rounded(d_first)
        put_lines(3, b, d_first, (FIRST_COL, LAST_COL))
        put_block(second, b, d_first)
        x_value = block(x_ref, b)
        left, right = column_shifts(x_value, halo_lines(0, b), halo_lines(1, b))
        pairs = (
            (d_first, left),
            (d_first, x_value),
            (d_first, right),
            (value, above),
            (value, first),
            (value, below),
        )
        return tuple(old + jnp.sum(a * c, axis=0) for old, (a, c) in zip(sums, pairs))

    tap_sums = lax.fori_loop(0, 6, first_back, tuple(jnp.zeros((8, channels), F32) for _ in range(6)))
    start_halos(3)
    for number, tap_sum in enumerate(tap_sums):
        row = ROW_TAPS + number
        small[row : row + 1, :channels] = jnp.sum(tap_sum, axis=0, keepdims=True)
    tile32[...] = jnp.zeros_like(tile32)
    line = 0
    for row, count in SMALL_ROWS:
        for number in range(count):
            tile32[line : line + 1, :] = small[row : row + 1, number * 128 : number * 128 + 128]
            line += 1
    slab[SMALL_AT] = tile32[:16].astype(BF16)
    slab[SMALL_AT + 1] = tile32[16:].astype(BF16)
    core_copy(2).start()

    def add_cores(number):
        at, size = regions[number]
        core_copy(number).wait_recv()

        def some(step, carry):
            here = at + step * 8
            total = slab[pl.ds(core * HALF + here, 8)].astype(F32)
            t1[pl.ds(here, 8)] = (total + core_rcv[pl.ds(here, 8)].astype(F32)).astype(BF16)
            return carry

        lax.fori_loop(0, size // 8, some, 0)

    def scatter(source, base, chunk, received, axis, count, me, stage):
        for step in range(1, count):
            to = (me + step) % count
            remote(
                source.at[pl.ds(base + to * chunk, chunk)],
                received.at[step - 1],
                stage,
                along(axis, step),
            ).start()

    def whole_wait(ref, sem):
        pltpu.make_async_copy(ref, ref, sem).wait()

    def add_all(source, at, received, target, to, stage):
        whole_wait(received, red_recv.at[stage])
        chunk = received.shape[1]
        total = source[pl.ds(at, chunk)].astype(F32)
        for number in range(received.shape[0]):
            total += received[number].astype(F32)
        target[pl.ds(to, chunk)] = total.astype(BF16)

    x_chunk, y_chunk, z_chunk = X_PART // nx, Y_PART // side, Z_PART // side
    add_cores(0)
    scatter(t1, 0, x_chunk, x_rcv, "x", nx, mx, 3)
    add_cores(1)
    scatter(t1, X_PART, y_chunk, y_rcv, "y", side, ty, 4)
    add_cores(2)
    scatter(t1, X_PART + Y_PART, z_chunk, z_rcv, "z", side, tx, 5)

    receive_halos(3)
    gather(4, 0, 3, west, "straight")
    gather(5, 1, 1, east, "straight")
    gather(6, 0, 0, top, "turned")
    gather(7, 1, 2, bottom, "turned")

    def input_back(b, carry):
        value = block(second, b)
        left, right = column_shifts(value, halo_lines(4, b), halo_lines(5, b))
        d_input = tap(0, 0) * right + tap(0, 1) * value + tap(0, 2) * left
        faces = d_input.reshape(2, 8, 8, channels)
        inner = faces[:, 1:7]
        north = faces[:, :1] + (tap(0, 0) * halo_lines(6, b))[:, None]
        south = faces[:, 7:] + (tap(0, 2) * halo_lines(7, b))[:, None]
        d_input = jnp.concatenate([north, inner, south], axis=1).reshape(16, 8, channels)
        put_block(gi_out, b, d_input + block(d_mix_s, b))
        return carry

    lax.fori_loop(0, 6, input_back, 0)

    y_at = x_chunk
    z_at = x_chunk + y_chunk
    half = x_chunk // 2
    add_all(t1, X_PART + ty * y_chunk, y_rcv, t2, y_at, 4)
    scatter(t2, y_at, unit, b2_rcv, "x", nx, mx, 8)
    add_all(t1, X_PART + Y_PART + tx * z_chunk, z_rcv, t2, z_at, 5)
    scatter(t2, z_at, unit, b3_rcv, "x", nx, mx, 9)
    add_all(t1, mx * x_chunk, x_rcv, t2, 0, 3)
    scatter(t2, 0, unit, b0_rcv, "y", side, ty, 6)
    scatter(t2, half, unit, b1_rcv, "z", side, tx, 7)

    def to_slot(source, at, received, slots, slot, piece, stage):
        whole_wait(received, red_recv.at[stage])
        total = source[pl.ds(at, unit)].astype(F32)
        for number in range(received.shape[0]):
            total += received[number].astype(F32)
        slots[slot, pl.ds(piece * unit, unit)] = total.astype(BF16)

    def spread_slot(slots, me, axis, stage):
        for step in range(1, side):
            remote(slots.at[me], slots.at[me], stage, along(axis, step)).start()

    to_slot(t2, y_at + mx * unit, b2_rcv, cz, tx, 1, 8)
    to_slot(t2, z_at + mx * unit, b3_rcv, cy, ty, 1, 9)
    to_slot(t2, ty * unit, b0_rcv, cz, tx, 0, 6)
    spread_slot(cz, tx, "z", 10)
    to_slot(t2, half + tx * unit, b1_rcv, cy, ty, 0, 7)
    spread_slot(cy, ty, "y", 11)

    base = core * HALF

    def sum_slots(slots, stage):
        whole_wait(slots.at[pl.ds(0, side - 1)], red_recv.at[stage])
        total = slots[0].astype(F32)
        for number in range(1, side):
            total += slots[number].astype(F32)
        return (total * norm_factor).astype(BF16)

    def share(at, size, axis, count, stage):
        piece = gathered.at[pl.ds(at, size)]
        for step in range(1, count):
            remote(piece, piece, stage, along(axis, step)).start()

    def await_shares(size, count, stage):
        whole_wait(gathered.at[pl.ds(0, size * (count - 1))], red_recv.at[stage])

    at0 = base + mx * x_chunk + ty * unit
    at1 = base + mx * x_chunk + half + tx * unit
    at2 = base + X_PART + ty * y_chunk + mx * unit
    at3 = base + X_PART + Y_PART + tx * z_chunk + mx * unit
    done = sum_slots(cz, 10)
    gathered[pl.ds(at0, unit)] = done[:unit]
    gathered[pl.ds(at2, unit)] = done[unit:]
    share(at0, unit, "y", side, 12)
    share(at2, unit, "x", nx, 14)
    done = sum_slots(cy, 11)
    gathered[pl.ds(at1, unit)] = done[:unit]
    gathered[pl.ds(at3, unit)] = done[unit:]
    share(at1, unit, "z", side, 13)
    share(at3, unit, "x", nx, 15)
    await_shares(unit, nx, 14)
    share(base + X_PART + ty * y_chunk, y_chunk, "y", side, 17)
    await_shares(unit, side, 12)
    await_shares(unit, side, 13)
    share(base + mx * x_chunk, x_chunk, "x", nx, 16)
    await_shares(unit, nx, 15)
    share(base + X_PART + Y_PART + tx * z_chunk, z_chunk, "z", side, 18)

    def core_back(number):
        at, size = regions[number]
        piece = gathered.at[pl.ds(base + at, size)]
        return remote(piece, piece, 19 + number, sibling)

    await_shares(x_chunk, nx, 16)
    core_back(0).start()
    await_shares(y_chunk, side, 17)
    core_back(1).start()
    await_shares(z_chunk, side, 18)
    core_back(2).start()
    for number in range(3):
        core_back(number).wait_recv()

    slab_out[...] = gathered[...]

    for exchange in range(4):
        finish_halo_sends(exchange)
    for number in range(3):
        core_copy(number).wait_send()
        core_back(number).wait_send()
    for ref, stage in (
        (x_rcv, 3),
        (y_rcv, 4),
        (z_rcv, 5),
        (b0_rcv, 6),
        (b1_rcv, 7),
        (b2_rcv, 8),
        (b3_rcv, 9),
        (cz.at[pl.ds(0, side - 1)], 10),
        (cy.at[pl.ds(0, side - 1)], 11),
        (gathered.at[pl.ds(0, unit * (side - 1))], 12),
        (gathered.at[pl.ds(0, unit * (side - 1))], 13),
        (gathered.at[pl.ds(0, unit * (nx - 1))], 14),
        (gathered.at[pl.ds(0, unit * (nx - 1))], 15),
        (gathered.at[pl.ds(0, x_chunk * (nx - 1))], 16),
        (gathered.at[pl.ds(0, y_chunk * (side - 1))], 17),
        (gathered.at[pl.ds(0, z_chunk * (side - 1))], 18),
    ):
        whole_wait(ref, red_send.at[stage])


def unpack_kernel(ns, gi, slab, ns_out, gi_out, up_out, down_out, gates_out, cand_out, small_out):
    ns_out[...] = ns[...]
    gi_out[...] = gi[...]

    def unpack(at, out, row_at, rows):
        across = out.shape[1] // 128
        for row in range(rows // 16):
            for column in range(across):
                out[
                    row_at + row * 16 : row_at + row * 16 + 16, column * 128 : column * 128 + 128
                ] = slab[at + row * across + column]

    unpack(CAND_AT, cand_out, 0, cand_out.shape[0])
    unpack(GATES_AT, gates_out, 0, gates_out.shape[0])
    unpack(DOWN_AT, down_out, 0, down_out.shape[0])
    unpack(UP_AT, up_out, 0, up_out.shape[0])
    small_out[:16, :] = slab[SMALL_AT]
    small_out[16:, :] = slab[SMALL_AT + 1]


def on_device(
    inputs,
    state,
    cotangent,
    adjacency,
    taps,
    gain,
    w_up,
    b_up,
    w_down,
    b_down,
    w_gates,
    b_gates,
    w_cand,
    b_cand,
):
    channels = inputs.shape[-1]
    wide = w_up.shape[1]
    tokens = FACES * SIDE * SIDE
    tile_count, date_count = lax.axis_size("tile"), lax.axis_size("date")
    side = 2 ** ((tile_count.bit_length() - 2) // 2)
    x_low = date_count // 2
    nx = 2 * x_low
    unit = 32 // (nx * side)
    norm_factor = float(tokens * tile_count * date_count) ** (-0.5)

    def row(value):
        return jnp.pad(value.astype(F32), (0, wide - value.shape[0]))

    par = jnp.stack(
        [row(b_up), row(b_gates)]
        + [row(taps[axis, number]) for axis in range(2) for number in range(3)]
        + [row(gain), row(b_down), row(b_cand)]
        + [jnp.zeros((wide,), F32)] * 5
    )
    vmem = pl.BlockSpec(memory_space=pltpu.VMEM)

    def buf(*shape):
        return pltpu.VMEM(shape, BF16)

    new_rows, grad_rows, slab = pl.pallas_call(
        functools.partial(level_kernel, side, x_low, norm_factor),
        name="level",
        out_shape=(
            jax.ShapeDtypeStruct((tokens, channels), BF16),
            jax.ShapeDtypeStruct((tokens, channels), BF16),
            jax.ShapeDtypeStruct((2 * HALF, 16, 128), BF16),
        ),
        in_specs=[pl.BlockSpec(memory_space=pltpu.SMEM)] + [vmem] * 8,
        out_specs=[vmem] * 3,
        scratch_shapes=[
            buf(4, 4, FACES * SIDE, channels),
            buf(4, 4, FACES * SIDE, channels),
            pltpu.VMEM((2, 25, SIDE, channels), F32),
            pltpu.VMEM((8, FACES, SIDE, channels), F32),
            pltpu.VMEM((tokens, channels), F32),
            pltpu.VMEM((tokens, channels), F32),
            buf(2 * channels, channels),
            buf(2 * channels, channels),
            buf(channels, channels),
            buf(channels, channels),
            buf(tokens, channels),
            buf(tokens, wide),
            buf(tokens, wide),
            buf(tokens, channels),
            buf(tokens, 2 * channels),
            buf(tokens, 2 * channels),
            buf(tokens, channels),
            buf(tokens, channels),
            pltpu.VMEM((16, wide), F32),
            pltpu.VMEM((32, 128), F32),
            buf(2 * HALF, 16, 128),
            buf(HALF, 16, 128),
            buf(HALF, 16, 128),
            buf(nx - 1, X_PART // nx, 16, 128),
            buf(side - 1, Y_PART // side, 16, 128),
            buf(side - 1, Z_PART // side, 16, 128),
            buf(X_PART // nx + Y_PART // side + Z_PART // side, 16, 128),
            buf(side - 1, unit, 16, 128),
            buf(side - 1, unit, 16, 128),
            buf(nx - 1, unit, 16, 128),
            buf(nx - 1, unit, 16, 128),
            buf(side, 2 * unit, 16, 128),
            buf(side, 2 * unit, 16, 128),
            buf(2 * HALF, 16, 128),
            pltpu.SemaphoreType.DMA((4, 4)),
            pltpu.SemaphoreType.DMA((4, 4)),
            pltpu.SemaphoreType.DMA((22,)),
            pltpu.SemaphoreType.DMA((22,)),
        ],
        compiler_params=pltpu.CompilerParams(
            collective_id=0, has_side_effects=True, vmem_limit_bytes=48 * 2**20
        ),
    )(
        adjacency.reshape(-1),
        inputs.reshape(tokens, channels),
        state.reshape(tokens, channels),
        cotangent.reshape(tokens, channels),
        par,
        w_up,
        w_down.T,
        w_gates,
        w_cand.T,
    )
    new_rows, grad_rows, g_up, g_down, g_gates, g_cand, g_small = pl.pallas_call(
        unpack_kernel,
        name="unpack",
        out_shape=(
            jax.ShapeDtypeStruct((tokens, channels), BF16),
            jax.ShapeDtypeStruct((tokens, channels), BF16),
            jax.ShapeDtypeStruct((channels, wide), BF16),
            jax.ShapeDtypeStruct((channels, wide), BF16),
            jax.ShapeDtypeStruct((2 * channels, 2 * channels), BF16),
            jax.ShapeDtypeStruct((channels, 2 * channels), BF16),
            jax.ShapeDtypeStruct((32, 128), BF16),
        ),
        in_specs=[vmem] * 3,
        out_specs=[vmem] * 7,
        compiler_params=pltpu.CompilerParams(vmem_limit_bytes=32 * 2**20),
    )(new_rows, grad_rows, slab)

    flat = g_small.reshape(-1)

    def piece(line, size):
        return flat[line * 128 : line * 128 + size]

    g_taps = g_small[9:21].reshape(2, 3, 256)[:, :, :channels]
    return (
        new_rows.reshape(inputs.shape),
        grad_rows.reshape(inputs.shape),
        g_taps,
        piece(21, channels),
        g_up,
        piece(0, wide),
        g_down.T,
        piece(23, channels),
        g_gates,
        piece(6, 2 * channels),
        g_cand.T,
        piece(25, channels),
    )


def solution(mesh):
    field = P("tile", "date", None, None, None, None)
    return jax.shard_map(
        on_device,
        mesh=mesh,
        in_specs=(field,) * 3 + (P(),) * 11,
        out_specs=(field,) * 2 + (P(),) * 10,
        check_vma=False,
    )
```

time: 470 us -> 95.7 us (0.20)
  waiting for transfers between devices: 135 us -> 0 us
  starting transfers between devices: 130 us -> 0 us
  blocking collectives: 121 us -> 0 us
  Pallas kernels: 0 us -> 81.2 us
  other arithmetic: 23 us -> 2.67 us
  matrix products: 19.1 us -> 0 us
  between operations: 15.9 us -> 0.77 us
  local copies, waits for them, and re-layouts: 24.4 us -> 10.7 us
    ppermute x36 -> x0, starting transfers between devices: 130 us -> none  [the longest x24 80.7 us: swapped(): return lax.ppermute(value, axis, pairs)]
    psum x1 -> x0, blocking collectives: 121 us -> none  [on_device(): lax.psum((grad_taps, gain_sum, up_sum, bup_sum, down_sum, bdown_sum, gate...]
    psum x1 -> x0, waiting for transfers between devices: 81.3 us -> none  [on_device(): lax.psum((grad_taps, gain_sum, up_sum, bup_sum, down_sum, bdown_sum, gate...]
    pallas_call x0 -> x2, Pallas kernels: none -> 81.2 us  [the longest x1 79.8 us: on_device(): pl.pallas_call(functools.partial(level_kernel, side, x_low, norm_factor),...]
    ppermute x36 -> x0, waiting for transfers between devices: 53.8 us -> none  [the longest x24 53.8 us: swapped(): return lax.ppermute(value, axis, pairs)]
    dot_general x28 -> x0, matrix products: 19.1 us -> none  [the longest x8 4.26 us: return_lines(): jnp.einsum('fg,fpc->gpc', relation, edge_lines, preferred_element_type=jn...]
    convert_element_type x23 -> x0, other arithmetic: 10.6 us -> none  [the longest x10 7.88 us: on_device(): (grad_piece * norm_factor).astype(jnp.bfloat16)]
    scatter-add x4 -> x0, local copies, waits for them, and re-layouts: 10.3 us -> none  [the longest x1 3.89 us: rows_back(): d_first.at[:, 0].add(taps_row[2] * to_north_row.astype(jnp.float32))]
  transfers between devices with their start and end apart: 37 -> 0, of which waited for: 19 -> 0; matrix products, arithmetic and copies ran while one was open for 7% -> 0% of each run, Pallas kernels for 0% -> 0%
where the time goes in v1:
time: 95.7 us; the launch traced here: 95.3 us
  Pallas kernels  81.2 us (85%)
  local copies, waits for them, and re-layouts  10.7 us (11%)
  other arithmetic  2.67 us (3%)
    pallas_call x1, Pallas kernels, on_device(): pl.pallas_call(functools.partial(level_kernel, side, x_low, norm_factor),...  79.8 us
    unnamed x16, local copies, waits for them, and re-layouts  7.2 us
    another operation x7, other arithmetic, on_device(): jnp.stack([row(b_up), row(b_gates)] + [row(taps[axis, number]) for axis i...  2.67 us

profile of v1, /device:TPU:1, one launch (start us, length us, event | category | flops | bytes accessed | tf_op | source)
XLA Modules:
  0.0 95.3 jit_solution(12519495853099652026)
XLA Ops:
  0.6 0.0 copy-start.3
  0.7 0.7 reshape.70
  1.4 0.8 slice_reduce_fusion
  2.2 0.7 pad_convert_fusion.2
  2.8 0.7 pad_convert_fusion.1
  3.5 0.7 pad_convert_fusion.9
  4.2 0.7 pad_convert_fusion
  5.0 0.1 stack.95.par
  5.1 0.8 copy.28
  5.9 0.1 reshape.62.adj
  6.0 0.0 copy-done.3
  6.0 0.0 copy-start
  6.0 1.0 %copy-done = bf16[1,1,12,8,8,192]{5,4,3,2,1,0:T(8,128)(2,1)S(1)} copy-done((bf16[1,1,12,8,8,192]{5,4,3,2,1,0:T(8,128)(2,1)S(1)}, bf16[1,1,12,8,8,192]{5,4,3,2,1,0:T(8,128)(2,1)}, u32[]{:S(2)}) %copy-start) | copy-done | bytes 294936
  7.0 1.0 %copy-done.1 = bf16[1,1,12,8,8,192]{5,4,3,2,1,0:T(8,128)(2,1)S(1)} copy-done((bf16[1,1,12,8,8,192]{5,4,3,2,1,0:T(8,128)(2,1)S(1)}, bf16[1,1,12,8,8,192]{5,4,3,2,1,0:T(8,128)(2,1)}, u32[]{:S(2)}) %copy-start.1) | copy-done | bytes 294936
  8.0 1.0 %copy-done.2 = bf16[1,1,12,8,8,192]{5,4,3,2,1,0:T(8,128)(2,1)S(1)} copy-done((bf16[1,1,12,8,8,192]{5,4,3,2,1,0:T(8,128)(2,1)S(1)}, bf16[1,1,12,8,8,192]{5,4,3,2,1,0:T(8,128)(2,1)}, u32[]{:S(2)}) %copy-start.2) | copy-done | bytes 294936
  9.0 1.0 %copy-done.4 = bf16[768,192]{0,1:T(8,128)(2,1)S(1)} copy-done((bf16[768,192]{0,1:T(8,128)(2,1)S(1)}, bf16[768,192]{0,1:T(8,128)(2,1)}, u32[]{:S(2)}) %copy-start.4) | copy-done | bytes 294936
  10.0 1.0 %copy-done.5 = bf16[384,384]{1,0:T(8,128)(2,1)S(1)} copy-done((bf16[384,384]{1,0:T(8,128)(2,1)S(1)}, bf16[384,384]{1,0:T(8,128)(2,1)}, u32[]{:S(2)}) %copy-start.5) | copy-done | bytes 294936
  10.9 0.9 copy-done.6
  11.8 79.8 %level.1 = (bf16[768,192]{1,0:T(8,128)(2,1)S(1)}, bf16[768,192]{1,0:T(8,128)(2,1)S(1)}, bf16[256,16,128]{2,1,0:T(8,128)(2,1)S(1)}) custom-call(s32[96]{0:T(128)S(1)} %reshape.62.adj, bf16[768,192]{1,0:T(8,128)(2,1)S(1)} %bitcast.15, bf16[768,192]{1,0:T(8,128)(2,1)S(1)} %bitcast.16, bf16[768,192]{1,0:T(8,128)(2,1)S(1)} %bitcast.17, f32[16,768]{1,0:T(8,128)S(1)} %stack.95.par, ...), custom_call_target="tpu_custom_call" | custom-call | tf_op jit(solution)/shard_map/level/pallas_call | solution.py:746
  91.6 1.4 %unpack.1 = (bf16[768,192]{1,0:T(8,128)(2,1)}, bf16[768,192]{1,0:T(8,128)(2,1)}, bf16[192,768]{1,0:T(8,128)(2,1)}, bf16[192,768]{1,0:T(8,128)(2,1)}, bf16[384,38...) custom-call(bf16[768,192]{1,0:T(8,128)(2,1)S(1)} %get-tuple-element.22.ns, ...), custom_call_target="tpu_custom_call" | custom-call | tf_op jit(solution)/shard_map/unpack/pallas_call | solution.py:810
  93.0 0.6 slice_bitcast_fusion.1
  93.6 0.5 fusion
  94.1 0.6 slice_bitcast_fusion
  94.7 0.6 copy.29
  (22 shorter events, 0.1 us)
Async XLA Ops:
  0.6 5.4 %copy-start.3 = (bf16[192,768]{1,0:T(8,128)(2,1)S(1)}, bf16[192,768]{1,0:T(8,128)(2,1)}, u32[]{:S(2)}) copy-start(bf16[192,768]{1,0:T(8,128)(2,1)} %w_up.1) | copy-start | bytes 884740
  6.0 1.0 %copy-start = (bf16[1,1,12,8,8,192]{5,4,3,2,1,0:T(8,128)(2,1)S(1)}, bf16[1,1,12,8,8,192]{5,4,3,2,1,0:T(8,128)(2,1)}, u32[]{:S(2)}) copy-start(bf16[1,1,12,8,8,192]{5,4,3,2,1,0:T(8,128)(2,1)} %param.14) | copy-start | bytes 884740
  7.0 1.0 %copy-start.1 = (bf16[1,1,12,8,8,192]{5,4,3,2,1,0:T(8,128)(2,1)S(1)}, bf16[1,1,12,8,8,192]{5,4,3,2,1,0:T(8,128)(2,1)}, u32[]{:S(2)}) copy-start(bf16[1,1,12,8,8,192]{5,4,3,2,1,0:T(8,128)(2,1)} %param.15) | copy-start | bytes 884740
  8.0 1.0 %copy-start.2 = (bf16[1,1,12,8,8,192]{5,4,3,2,1,0:T(8,128)(2,1)S(1)}, bf16[1,1,12,8,8,192]{5,4,3,2,1,0:T(8,128)(2,1)}, u32[]{:S(2)}) copy-start(bf16[1,1,12,8,8,192]{5,4,3,2,1,0:T(8,128)(2,1)} %param.16) | copy-start | bytes 884740
  9.0 1.0 %copy-start.4 = (bf16[768,192]{0,1:T(8,128)(2,1)S(1)}, bf16[768,192]{0,1:T(8,128)(2,1)}, u32[]{:S(2)}) copy-start(bf16[768,192]{0,1:T(8,128)(2,1)} %param.22) | copy-start | bytes 884740
  10.0 1.0 %copy-start.5 = (bf16[384,384]{1,0:T(8,128)(2,1)S(1)}, bf16[384,384]{1,0:T(8,128)(2,1)}, u32[]{:S(2)}) copy-start(bf16[384,384]{1,0:T(8,128)(2,1)} %w_gates.1) | copy-start | bytes 884740
  10.9 0.9 copy-start.6

commit v2 on v1

v2 whole, which is shorter than its diff:
```python
import functools
import math

import jax
import jax.numpy as jnp
from jax import lax
from jax.experimental import pallas as pl
from jax.experimental.pallas import tpu as pltpu
from jax.sharding import PartitionSpec as P

EPSILON = 1e-06
MESH = pl.DeviceIdType.MESH
F32 = jnp.float32
BF16 = jnp.bfloat16
FACES = 12
SIDE = 8
HALF = 128
REGION = 64
FIRST_ROW, LAST_ROW, FIRST_COL, LAST_COL = range(4)
GELU_A = math.sqrt(2.0 / math.pi)
GELU_B = 0.044715
ROW_BUP, ROW_BGATES, ROW_TAPS, ROW_GAIN, ROW_BDOWN, ROW_BCAND = 0, 1, 2, 8, 9, 10
SMALL_ROWS = ((0, 6), (1, 3)) + tuple((row, 2) for row in range(2, 11))
CAND_AT, GATES_AT, DOWN_AT, UP_AT, SMALL_AT = 0, 36, 108, 180, 252


def nn(left, right):
    return jnp.dot(left, right, preferred_element_type=F32)


def nt(left, right):
    return lax.dot_general(left, right, (((1,), (1,)), ((), ())), preferred_element_type=F32)


def tn(left, right):
    return lax.dot_general(left, right, (((0,), (0,)), ((), ())), preferred_element_type=F32)


def sigmoid(value):
    return 0.5 + 0.5 * jnp.tanh(0.5 * value)


def tile_place(number):
    if 64 <= number < 128:
        return number + 64
    if 128 <= number < 192:
        return number - 64
    return number


def store_tiles(slab, at, matrix):
    rows, columns = matrix.shape
    packed = matrix.astype(BF16)
    across = columns // 128
    for row in range(rows // 16):
        for column in range(across):
            slab[tile_place(at + row * across + column)] = packed[
                row * 16 : row * 16 + 16, column * 128 : column * 128 + 128
            ]


def level_kernel(
    side,
    x_low,
    norm_factor,
    adj_in,
    x_in,
    h_in,
    g_in,
    taps_in,
    gain_in,
    b_up_in,
    b_down_in,
    b_gates_in,
    b_cand_in,
    w_up_in,
    w_down_in,
    w_gates_in,
    w_cand_in,
    ns_out,
    gi_out,
    slab_out,
    small_out,
    adj,
    x_ref,
    h_ref,
    g_ref,
    taps_ref,
    gain_ref,
    b_up_ref,
    b_down_ref,
    b_gates_ref,
    b_cand_ref,
    w_up,
    w_down_t,
    w_gates,
    w_cand_t,
    par,
    snd,
    rcv,
    pool,
    halo,
    columns,
    field,
    d_sec,
    d_first_s,
    wg_u,
    wg_r,
    wc_m,
    wc_r,
    prior_s,
    normed_s,
    hid_s,
    d_pre_s,
    d_mix_s,
    d_gate_s,
    joined_s,
    d_cand_s,
    small,
    tile32,
    small_c,
    small_x,
    small_y,
    small_z,
    slab,
    core_rcv,
    t1,
    xy_rcv,
    xz_rcv,
    cz,
    cy,
    gathered,
    load_sem,
    halo_send,
    halo_recv,
    red_send,
    red_recv,
):
    channels = x_ref.shape[3]
    nx = 2 * x_low
    unit = REGION // (nx * side)
    tile = lax.axis_index("tile")
    date = lax.axis_index("date")
    place_of_tile = lax.div(tile, 2)
    ty, tx = lax.div(place_of_tile, side), lax.rem(place_of_tile, side)
    core = lax.rem(date, 2)
    mx = lax.rem(tile, 2) * x_low + lax.div(date, 2)

    def device(x, y, z, c):
        return ((y * side + z) * 2 + lax.div(x, x_low), lax.rem(x, x_low) * 2 + c)

    def moved(dx, dy, dz):
        x = lax.rem(mx + dx, nx) if dx else mx
        y = lax.rem(ty + dy, side) if dy else ty
        z = lax.rem(tx + dz, side) if dz else tx
        return x, y, z

    def offset(dx, dy, dz):
        return device(*moved(dx, dy, dz), core)

    sibling = device(mx, ty, tx, 1 - core)
    across = device(mx, tx, ty, core)
    top, bottom = ty == 0, ty == side - 1
    west, east = tx == 0, tx == side - 1
    has_across = jnp.logical_and(
        ty != tx,
        jnp.logical_or(jnp.logical_or(top, bottom), jnp.logical_or(west, east)),
    )

    def far(step):
        dx, dy, dz = step
        return min(dx, nx - dx) + min(dy, side - dy) + min(dz, side - dz)

    xy_steps = [(dx, dy, 0) for dx in range(nx) for dy in range(side) if dx or dy]
    xz_steps = [(dx, 0, dz) for dx in range(nx) for dz in range(side) if dx or dz]
    xy_steps.sort(key=far, reverse=True)
    xz_steps.sort(key=far, reverse=True)
    x_steps = [(dx, 0, 0) for dx in range(1, nx)]
    y_steps = [(0, dy, 0) for dy in range(1, side)]
    z_steps = [(0, 0, dz) for dz in range(1, side)]

    barrier = pltpu.get_barrier_semaphore()

    @pl.when(has_across)
    def _():
        pl.semaphore_signal(barrier, inc=1, device_id=across, device_id_type=MESH)

    peers = [offset(*step) for step in xy_steps]
    peers += [offset(*step) for step in xz_steps if step[2]]
    peers.append(sibling)
    for peer in peers:
        pl.semaphore_signal(barrier, inc=1, device_id=peer, device_id_type=MESH)

    loads = [
        pltpu.make_async_copy(src, dst, load_sem.at[number])
        for number, (src, dst) in enumerate(
            (
                (x_in, x_ref),
                (taps_in, taps_ref),
                (adj_in, adj),
                (w_gates_in, w_gates),
                (w_cand_in, w_cand_t),
                (gain_in, gain_ref),
                (b_up_in, b_up_ref),
                (b_down_in, b_down_ref),
                (b_gates_in, b_gates_ref),
                (b_cand_in, b_cand_ref),
                (w_up_in, w_up),
                (w_down_in, w_down_t),
                (h_in, h_ref),
                (g_in, g_ref),
            )
        )
    ]
    for load in loads:
        load.start()

    def tap(axis, number):
        row = ROW_TAPS + 3 * axis + number
        return par[row : row + 1, :channels].reshape(1, 1, channels)

    def set_columns(value, i):
        columns[0, :, pl.ds(i, 1), :] = value[:, 0:1, :]
        columns[1, :, pl.ds(i, 1), :] = value[:, 7:8, :]

    def put_line(exchange, kind, value):
        snd[exchange, kind] = value.reshape(FACES * SIDE, channels).astype(BF16)

    def put_columns(exchange):
        put_line(exchange, FIRST_COL, columns[0])
        put_line(exchange, LAST_COL, columns[1])

    loads[0].wait()

    def x_row(i):
        return x_ref[:, pl.ds(i, 1)].astype(F32).reshape(FACES, SIDE, channels)

    def x_lines(i, carry):
        set_columns(x_row(i), i)
        return carry

    lax.fori_loop(0, 8, x_lines, 0)
    put_columns(0)
    put_line(0, FIRST_ROW, x_row(0))
    put_line(0, LAST_ROW, x_row(7))

    @pl.when(has_across)
    def _():
        pl.semaphore_wait(barrier, len(peers) + 1)

    @pl.when(jnp.logical_not(has_across))
    def _():
        pl.semaphore_wait(barrier, len(peers))

    def halo_copies(exchange):
        on_columns = exchange in (0, 3)
        rows_turn = exchange in (0, 2)
        last, first = (LAST_COL, FIRST_COL) if on_columns else (LAST_ROW, FIRST_ROW)
        t_first, t_last = (FIRST_ROW, LAST_ROW) if rows_turn else (FIRST_COL, LAST_COL)
        row_first = jnp.logical_and(top, jnp.logical_not(west))
        row_last = jnp.logical_and(bottom, jnp.logical_not(east))
        col_first = jnp.logical_and(west, jnp.logical_not(top))
        col_last = jnp.logical_and(east, jnp.logical_not(bottom))
        if rows_turn:
            sends, receives = (row_first, row_last), (col_first, col_last)
        else:
            sends, receives = (col_first, col_last), (row_first, row_last)
        if on_columns:
            ahead, behind = offset(0, 0, 1), offset(0, 0, side - 1)
        else:
            ahead, behind = offset(0, 1, 0), offset(0, side - 1, 0)
        targets = (ahead, behind, across, across)
        return [
            (
                pltpu.make_async_remote_copy(
                    src_ref=snd.at[exchange, line],
                    dst_ref=rcv.at[exchange, kind],
                    send_sem=halo_send.at[exchange, kind],
                    recv_sem=halo_recv.at[exchange, kind],
                    device_id=target,
                    device_id_type=MESH,
                ),
                None if kind < 2 else sends[kind - 2],
                None if kind < 2 else receives[kind - 2],
                line,
            )
            for kind, (line, target) in enumerate(zip((last, first, t_first, t_last), targets))
        ]

    def start_halos(exchange):
        for copy, sends, _, _ in reversed(halo_copies(exchange)):
            if sends is None:
                copy.start()
            else:
                pl.when(sends)(copy.start)

    def finish_halo_sends(exchange):
        for copy, sends, _, _ in halo_copies(exchange):
            if sends is None:
                copy.wait_send()
            else:
                pl.when(sends)(copy.wait_send)

    def receive_halos(exchange):
        copies = halo_copies(exchange)
        corners = (jnp.logical_and(top, west), jnp.logical_and(bottom, east))

        def spread(ref, at):
            pool[at[0], at[1] : at[1] + 12] = (
                ref[...].astype(F32).reshape(FACES, SIDE, channels)
            )

        for kind, (copy, _, receives, line) in enumerate(copies):
            if kind < 2:
                copy.wait_recv()
                spread(rcv.at[exchange, kind], (kind, 0))
            else:

                @pl.when(receives)
                def _():
                    copy.wait_recv()
                    spread(rcv.at[exchange, kind], (kind - 2, 12))

                @pl.when(corners[kind - 2])
                def _():
                    spread(snd.at[exchange, line], (kind - 2, 12))

    def gather(to, which, edge, on_border, mode):
        for face in range(FACES):
            neighbour = adj[edge, 0, face]
            turned = adj[edge, 1, face] != (edge + 2) % 4
            if mode == "both":
                there = jnp.where(turned, 12 + neighbour, neighbour)
                index = jnp.where(on_border, there, face)
            elif mode == "straight":
                index = jnp.where(on_border, jnp.where(turned, 24, neighbour), face)
            else:
                index = jnp.where(jnp.logical_and(on_border, turned), 12 + neighbour, 24)
            to[face] = pool[which, index]

    place = lax.broadcasted_iota(jnp.int32, (FACES, SIDE, channels), 1)

    def upright(which, i):
        return jnp.broadcast_to(halo[which, :, pl.ds(i, 1), :], (FACES, SIDE, channels))

    def column_shifts(value, west_lines, east_lines, i):
        left = jnp.where(place == 0, upright(west_lines, i), pltpu.roll(value, 1, 1))
        right = jnp.where(place == 7, upright(east_lines, i), pltpu.roll(value, 7, 1))
        return left, right

    def rounded(value):
        return value.astype(BF16).astype(F32)

    start_halos(0)
    pool[...] = jnp.zeros_like(pool)
    small[...] = jnp.zeros_like(small)
    slab[SMALL_AT : 2 * HALF] = jnp.zeros((2 * HALF - SMALL_AT, 16, 128), BF16)
    for load in loads[1:10]:
        load.wait()
    for axis in range(2):
        for number in range(3):
            row = ROW_TAPS + 3 * axis + number
            par[row : row + 1, :channels] = taps_ref[number, axis : axis + 1, :].astype(F32)
    for row, ref in (
        (ROW_GAIN, gain_ref),
        (ROW_BUP, b_up_ref),
        (ROW_BDOWN, b_down_ref),
        (ROW_BGATES, b_gates_ref),
        (ROW_BCAND, b_cand_ref),
    ):
        size = ref.shape[0]
        par[row : row + 1, :size] = ref[...].astype(F32).reshape(1, size)
    wg_u[...] = w_gates[:, :channels]
    wg_r[...] = w_gates[:, channels:]
    wc_m[...] = w_cand_t[:, :channels]
    wc_r[...] = w_cand_t[:, channels:]
    for load in loads[10:]:
        load.wait()

    receive_halos(0)
    gather(halo.at[0], 0, 3, west, "both")
    gather(halo.at[1], 1, 1, east, "both")

    def first_pass(i, carry):
        value = x_row(i)
        left, right = column_shifts(value, 0, 1, i)
        first = rounded(tap(0, 0) * left + tap(0, 1) * value + tap(0, 2) * right)
        field[i + 1] = first
        set_columns(first, i)
        return carry

    lax.fori_loop(0, 8, first_pass, 0)
    put_columns(1)
    put_line(1, FIRST_ROW, field[1])
    put_line(1, LAST_ROW, field[8])
    start_halos(1)

    def vector(row, start, size):
        return par[row : row + 1, start : start + size]

    def cell(b, sums):
        rows = pl.ds(pl.multiple_of(b * 192, 192), 192)
        pair = (2 * b + 1, lax.rem(2 * b + 2, 8))

        @pl.when(b == 3)
        def _():
            receive_halos(1)
            gather(field.at[0], 0, 0, top, "both")
            gather(field.at[9], 1, 2, bottom, "both")

        def both(read):
            return jnp.concatenate(
                [read(i).reshape(FACES * SIDE, channels) for i in pair], axis=0
            )

        def second_row(i):
            return tap(1, 0) * field[i] + tap(1, 1) * field[i + 1] + tap(1, 2) * field[i + 2]

        def row_of(ref):
            return lambda i: ref[:, pl.ds(i, 1)].astype(F32)

        gain = vector(ROW_GAIN, 0, channels)
        centred = both(second_row)
        centred = centred - jnp.mean(centred, axis=-1, keepdims=True)
        inv_scale = lax.rsqrt(jnp.mean(centred * centred, axis=-1, keepdims=True) + EPSILON)
        standard = centred * inv_scale
        normed = (standard * gain).astype(BF16)
        normed_s[rows, :] = normed
        pre = nn(normed, w_up[...]) + vector(ROW_BUP, 0, w_up.shape[1])
        square = pre * pre
        curve = jnp.tanh(GELU_A * pre * (1.0 + GELU_B * square))
        hid = (0.5 * pre * (1.0 + curve)).astype(BF16)
        hid_s[rows, :] = hid
        slope = 0.5 * (1.0 + curve) + (0.5 * GELU_A) * pre * (1.0 - curve * curve) * (
            1.0 + 3.0 * GELU_B * square
        )
        mixed = (
            both(row_of(x_ref)) + nt(hid, w_down_t[...]) + vector(ROW_BDOWN, 0, channels)
        ).astype(BF16)
        joined_s[rows, :channels] = mixed
        prior = both(row_of(h_ref))
        prior_b = prior.astype(BF16)
        prior_s[rows, :] = prior_b
        update = sigmoid(
            nn(mixed, wg_u[:channels])
            + nn(prior_b, wg_u[channels:])
            + vector(ROW_BGATES, 0, channels)
        )
        reset = sigmoid(
            nn(mixed, wg_r[:channels])
            + nn(prior_b, wg_r[channels:])
            + vector(ROW_BGATES, channels, channels)
        )
        reset_state = (reset * prior).astype(BF16)
        joined_s[rows, channels:] = reset_state
        candidate = jnp.tanh(
            nt(mixed, wc_m[...]) + nt(reset_state, wc_r[...]) + vector(ROW_BCAND, 0, channels)
        )
        new = ((1.0 - update) * candidate + update * prior).astype(BF16)
        upstream = both(row_of(g_ref))
        kept = upstream * (1.0 - update)
        d_cand = (kept * (1.0 - candidate * candidate)).astype(BF16)
        d_cand_s[rows, :] = d_cand
        d_update = (kept * (prior - candidate) * update).astype(BF16)
        d_reset = (nn(d_cand, wc_r[...]) * prior * reset * (1.0 - reset)).astype(BF16)
        d_gate_s[rows, :channels] = d_update
        d_gate_s[rows, channels:] = d_reset
        d_mixed = (
            nn(d_cand, wc_m[...])
            + nt(d_update, wg_u[:channels])
            + nt(d_reset, wg_r[:channels])
        ).astype(BF16)
        d_mix_s[rows, :] = d_mixed
        d_pre = (nn(d_mixed, w_down_t[...]) * slope).astype(BF16)
        d_pre_s[rows, :] = d_pre
        d_normed = nt(d_pre, w_up[...])
        d_standard = d_normed * gain
        d_second = rounded(
            inv_scale
            * (
                d_standard
                - jnp.mean(d_standard, axis=-1, keepdims=True)
                - standard * jnp.mean(d_standard * standard, axis=-1, keepdims=True)
            )
        )
        new = new.astype(F32)
        for number, i in enumerate(pair):
            part = slice(number * 96, number * 96 + 96)
            d_sec[i + 1] = d_second[part].reshape(FACES, SIDE, channels)
            ns_out[:, pl.ds(i, 1)] = (
                new[part].reshape(FACES, 1, SIDE, channels).astype(BF16)
            )

        def total(value):
            return jnp.sum(value.astype(F32), axis=0, keepdims=True)

        extras = (
            total(d_pre),
            total(d_update),
            total(d_reset),
            total(d_normed * standard),
            total(d_mixed),
            total(d_cand),
        )
        return tuple(old + new_sum for old, new_sum in zip(sums, extras))

    zeros = jnp.zeros((1, channels), F32)
    sums = lax.fori_loop(
        0,
        4,
        cell,
        (jnp.zeros((1, w_up.shape[1]), F32), zeros, zeros, zeros, zeros, zeros),
    )
    put_line(2, FIRST_ROW, d_sec[1])
    put_line(2, LAST_ROW, d_sec[8])
    start_halos(2)
    small[ROW_BUP : ROW_BUP + 1, :] = sums[0]
    small[ROW_BGATES : ROW_BGATES + 1, :channels] = sums[1]
    small[ROW_BGATES : ROW_BGATES + 1, channels : 2 * channels] = sums[2]
    small[ROW_GAIN : ROW_GAIN + 1, :channels] = sums[3]
    small[ROW_BDOWN : ROW_BDOWN + 1, :channels] = sums[4]
    small[ROW_BCAND : ROW_BCAND + 1, :channels] = sums[5]

    def remote(src, dst, stage, target):
        return pltpu.make_async_remote_copy(
            src_ref=src,
            dst_ref=dst,
            send_sem=red_send.at[stage],
            recv_sem=red_recv.at[stage],
            device_id=target,
            device_id_type=MESH,
        )

    def whole_wait(ref, sem):
        pltpu.make_async_copy(ref, ref, sem).wait()

    def core_copy(region):
        return remote(
            slab.at[pl.ds((1 - core) * HALF + region * REGION, REGION)],
            core_rcv.at[pl.ds(region * REGION, REGION)],
            region,
            sibling,
        )

    store_tiles(slab, CAND_AT, tn(d_cand_s[...], joined_s[...]))
    store_tiles(slab, GATES_AT, tn(joined_s[:, :channels], d_gate_s[...]))
    store_tiles(slab, GATES_AT + 36, tn(prior_s[...], d_gate_s[...]))
    store_tiles(slab, DOWN_AT, tn(d_mix_s[...], hid_s[...]))
    core_copy(0).start()
    store_tiles(slab, UP_AT, tn(normed_s[...], d_pre_s[...]))
    core_copy(1).start()

    def add_cores(region):
        core_copy(region).wait_recv()

        def some(step, carry):
            here = region * REGION + step * 8
            total = slab[pl.ds(core * HALF + here, 8)].astype(F32)
            t1[pl.ds(here, 8)] = (total + core_rcv[pl.ds(here, 8)].astype(F32)).astype(BF16)
            return carry

        lax.fori_loop(0, REGION // 8, some, 0)

    def scatter(region, steps, received, stage):
        for number, step in enumerate(steps):
            x, y, z = moved(*step)
            other = z if region else y
            remote(
                t1.at[pl.ds(region * REGION + (x * side + other) * unit, unit)],
                received.at[number],
                stage,
                device(x, y, z, core),
            ).start()

    add_cores(0)
    scatter(0, xy_steps, xy_rcv, 2)
    add_cores(1)
    scatter(1, xz_steps, xz_rcv, 3)

    receive_halos(2)
    gather(d_sec.at[0], 0, 0, top, "straight")
    gather(d_sec.at[9], 1, 2, bottom, "straight")
    gather(halo.at[2], 0, 3, west, "turned")
    gather(halo.at[3], 1, 1, east, "turned")

    def first_back(i, sums):
        value = d_sec[i + 1]
        d_first = tap(1, 0) * d_sec[i + 2] + tap(1, 1) * value + tap(1, 2) * d_sec[i]
        d_first += jnp.where(place == 0, tap(1, 0) * upright(2, i), 0.0)
        d_first += jnp.where(place == 7, tap(1, 2) * upright(3, i), 0.0)
        d_first = rounded(d_first)
        d_first_s[i] = d_first
        set_columns(d_first, i)
        x_value = x_row(i)
        left, right = column_shifts(x_value, 0, 1, i)
        pairs = (
            (d_first, left),
            (d_first, x_value),
            (d_first, right),
            (value, field[i]),
            (value, field[i + 1]),
            (value, field[i + 2]),
        )
        return tuple(old + jnp.sum(a * c, axis=0) for old, (a, c) in zip(sums, pairs))

    tap_sums = lax.fori_loop(
        0, 8, first_back, tuple(jnp.zeros((SIDE, channels), F32) for _ in range(6))
    )
    put_columns(3)
    start_halos(3)

    for number, tap_sum in enumerate(tap_sums):
        row = ROW_TAPS + number
        small[row : row + 1, :channels] = jnp.sum(tap_sum, axis=0, keepdims=True)
    tile32[...] = jnp.zeros_like(tile32)
    line = 0
    for row, count in SMALL_ROWS:
        for number in range(count):
            tile32[line : line + 1, :] = small[row : row + 1, number * 128 : number * 128 + 128]
            line += 1
    small_c[0] = tile32[...].astype(BF16)
    small_core = remote(small_c.at[0], small_c.at[1], 4, sibling)
    small_core.start()

    def spread_slot(slots, me, steps, stage):
        for step in steps:
            remote(slots.at[me], slots.at[me], stage, offset(*step)).start()

    def sum_slots(slots, stage):
        count = slots.shape[0]
        whole_wait(slots.at[pl.ds(0, count - 1)], red_recv.at[stage])
        total = slots[0].astype(F32)
        for number in range(1, count):
            total += slots[number].astype(F32)
        return total

    def add_scattered(region, at, received, slots, slot, stage):
        whole_wait(received, red_recv.at[stage])
        total = t1[pl.ds(region * REGION + at * unit, unit)].astype(F32)
        for number in range(received.shape[0]):
            total += received[number].astype(F32)
        slots[slot] = total.astype(BF16)

    add_scattered(0, mx * side + ty, xy_rcv, cz, tx, 2)
    spread_slot(cz, tx, z_steps, 5)
    add_scattered(1, mx * side + tx, xz_rcv, cy, ty, 3)
    spread_slot(cy, ty, y_steps, 6)
    small_core.wait_recv()
    small_x[mx] = (small_c[0].astype(F32) + small_c[1].astype(F32)).astype(BF16)
    spread_slot(small_x, mx, x_steps, 7)
    small_y[ty] = sum_slots(small_x, 7).astype(BF16)
    spread_slot(small_y, ty, y_steps, 8)

    base = core * HALF

    def share(region, at, slots, stage, steps, out_stage):
        at = base + region * REGION + at * unit
        gathered[pl.ds(at, unit)] = (sum_slots(slots, stage) * norm_factor).astype(BF16)
        piece = gathered.at[pl.ds(at, unit)]
        for step in steps:
            remote(piece, piece, out_stage, offset(*step)).start()

    share(0, mx * side + ty, cz, 5, xy_steps, 10)
    share(1, mx * side + tx, cy, 6, xz_steps, 11)

    receive_halos(3)
    gather(halo.at[2], 0, 3, west, "straight")
    gather(halo.at[3], 1, 1, east, "straight")
    gather(halo.at[4], 0, 0, top, "turned")
    gather(halo.at[5], 1, 2, bottom, "turned")

    def input_back(i, carry):
        value = d_first_s[i]
        left, right = column_shifts(value, 2, 3, i)
        d_input = tap(0, 0) * right + tap(0, 1) * value + tap(0, 2) * left
        on_top = jnp.where(i == 0, 1.0, 0.0)
        on_bottom = jnp.where(i == 7, 1.0, 0.0)
        d_input += on_top * (tap(0, 0) * halo[4]) + on_bottom * (tap(0, 2) * halo[5])
        at = pl.multiple_of(lax.rem(i + 7, 8) * 96, 96)
        d_mixed = d_mix_s[pl.ds(at, 96), :].astype(F32).reshape(FACES, SIDE, channels)
        gi_out[:, pl.ds(i, 1)] = (
            (d_input + d_mixed).reshape(FACES, 1, SIDE, channels).astype(BF16)
        )
        return carry

    lax.fori_loop(0, 8, input_back, 0)

    small_z[tx] = sum_slots(small_y, 8).astype(BF16)
    spread_slot(small_z, tx, z_steps, 9)
    small_out[...] = sum_slots(small_z, 9) * norm_factor

    def core_back(region):
        piece = gathered.at[pl.ds(base + region * REGION, REGION)]
        return remote(piece, piece, 12 + region, sibling)

    shares = nx * side - 1
    for region in range(2):
        whole_wait(gathered.at[pl.ds(0, unit * shares)], red_recv.at[10 + region])
        core_back(region).start()
    for region in range(2):
        core_back(region).wait_recv()
    slab_out[...] = gathered[...]

    for exchange in range(4):
        finish_halo_sends(exchange)
    small_core.wait_send()
    for region in range(2):
        core_copy(region).wait_send()
        core_back(region).wait_send()
    for ref, stage in (
        (xy_rcv, 2),
        (xz_rcv, 3),
        (cz.at[pl.ds(0, side - 1)], 5),
        (cy.at[pl.ds(0, side - 1)], 6),
        (small_x.at[pl.ds(0, nx - 1)], 7),
        (small_y.at[pl.ds(0, side - 1)], 8),
        (small_z.at[pl.ds(0, side - 1)], 9),
        (gathered.at[pl.ds(0, unit * shares)], 10),
        (gathered.at[pl.ds(0, unit * shares)], 11),
    ):
        whole_wait(ref, red_send.at[stage])


def unpack_kernel(
    ns,
    gi,
    slab,
    small,
    ns_out,
    gi_out,
    taps_out,
    gain_out,
    up_out,
    b_up_out,
    down_out,
    b_down_out,
    gates_out,
    b_gates_out,
    cand_out,
    b_cand_out,
):
    ns_out[...] = ns[...]
    gi_out[...] = gi[...]

    def unpack(at, out):
        across = out.shape[1] // 128
        for row in range(out.shape[0] // 16):
            for column in range(across):
                out[row * 16 : row * 16 + 16, column * 128 : column * 128 + 128] = slab[
                    tile_place(at + row * across + column)
                ]

    unpack(CAND_AT, cand_out)
    unpack(GATES_AT, gates_out)
    unpack(DOWN_AT, down_out)
    unpack(UP_AT, up_out)

    def row_at(line, size):
        pieces = [small[line + number : line + number + 1, :] for number in range(-(-size // 128))]
        return jnp.concatenate(pieces, axis=1)[:, :size].astype(BF16)

    channels = gain_out.shape[0]
    for axis in range(2):
        for number in range(3):
            taps_out[number, axis : axis + 1, :] = row_at(9 + 2 * (3 * axis + number), channels)
    for out, line in (
        (b_up_out, 0),
        (b_gates_out, 6),
        (gain_out, 21),
        (b_down_out, 23),
        (b_cand_out, 25),
    ):
        out[...] = row_at(line, out.shape[0]).reshape(out.shape)


def on_device(
    inputs,
    state,
    cotangent,
    adjacency,
    taps,
    gain,
    w_up,
    b_up,
    w_down,
    b_down,
    w_gates,
    b_gates,
    w_cand,
    b_cand,
):
    channels = inputs.shape[-1]
    wide = w_up.shape[1]
    tokens = FACES * SIDE * SIDE
    lines = FACES * SIDE
    tile_count, date_count = lax.axis_size("tile"), lax.axis_size("date")
    side = 2 ** ((tile_count.bit_length() - 2) // 2)
    x_low = date_count // 2
    nx = 2 * x_low
    unit = REGION // (nx * side)
    norm_factor = float(tokens * tile_count * date_count) ** (-0.5)
    vmem = pl.BlockSpec(memory_space=pltpu.VMEM)
    hbm = pl.BlockSpec(memory_space=pltpu.HBM)
    grid_shape = (FACES, SIDE, SIDE, channels)

    def buf(*shape):
        return pltpu.VMEM(shape, BF16)

    def wide_buf(*shape):
        return pltpu.VMEM(shape, F32)

    def arr(*shape):
        return jax.ShapeDtypeStruct(shape, BF16)

    shares = nx * side - 1
    new_rows, grad_rows, slab, small = pl.pallas_call(
        functools.partial(level_kernel, side, x_low, norm_factor),
        name="level",
        out_shape=(
            arr(*grid_shape),
            arr(*grid_shape),
            arr(2 * HALF, 16, 128),
            jax.ShapeDtypeStruct((32, 128), F32),
        ),
        in_specs=[hbm] * 14,
        out_specs=[vmem] * 4,
        scratch_shapes=[
            pltpu.SMEM((4, 2, FACES), jnp.int32),
            buf(*grid_shape),
            buf(*grid_shape),
            buf(*grid_shape),
            buf(3, 2, channels),
            buf(channels),
            buf(wide),
            buf(channels),
            buf(2 * channels),
            buf(channels),
            buf(channels, wide),
            buf(channels, wide),
            buf(2 * channels, 2 * channels),
            buf(channels, 2 * channels),
            wide_buf(16, wide),
            buf(4, 4, lines, channels),
            buf(4, 4, lines, channels),
            wide_buf(2, 25, SIDE, channels),
            wide_buf(6, FACES, SIDE, channels),
            wide_buf(2, FACES, SIDE, channels),
            wide_buf(10, FACES, SIDE, channels),
            wide_buf(10, FACES, SIDE, channels),
            wide_buf(8, FACES, SIDE, channels),
            buf(2 * channels, channels),
            buf(2 * channels, channels),
            buf(channels, channels),
            buf(channels, channels),
            buf(tokens, channels),
            buf(tokens, channels),
            buf(tokens, wide),
            buf(tokens, wide),
            buf(tokens, channels),
            buf(tokens, 2 * channels),
            buf(tokens, 2 * channels),
            buf(tokens, channels),
            wide_buf(16, wide),
            wide_buf(32, 128),
            buf(2, 32, 128),
            buf(nx, 32, 128),
            buf(side, 32, 128),
            buf(side, 32, 128),
            buf(2 * HALF, 16, 128),
            buf(HALF, 16, 128),
            buf(HALF, 16, 128),
            buf(shares, unit, 16, 128),
            buf(shares, unit, 16, 128),
            buf(side, unit, 16, 128),
            buf(side, unit, 16, 128),
            buf(2 * HALF, 16, 128),
            pltpu.SemaphoreType.DMA((14,)),
            pltpu.SemaphoreType.DMA((4, 4)),
            pltpu.SemaphoreType.DMA((4, 4)),
            pltpu.SemaphoreType.DMA((14,)),
            pltpu.SemaphoreType.DMA((14,)),
        ],
        compiler_params=pltpu.CompilerParams(
            collective_id=0, has_side_effects=True, vmem_limit_bytes=60 * 2**20
        ),
    )(
        adjacency.transpose(1, 2, 0),
        inputs.reshape(grid_shape),
        state.reshape(grid_shape),
        cotangent.reshape(grid_shape),
        taps.transpose(1, 0, 2),
        gain,
        b_up,
        b_down,
        b_gates,
        b_cand,
        w_up,
        w_down.T,
        w_gates,
        w_cand.T,
    )
    new_rows, grad_rows, g_taps, g_gain, g_up, g_bup, g_down, g_bdown, g_gates, g_bgates, g_cand, g_bcand = (
        pl.pallas_call(
            unpack_kernel,
            name="unpack",
            out_shape=(
                arr(*grid_shape),
                arr(*grid_shape),
                arr(3, 2, channels),
                arr(channels),
                arr(channels, wide),
                arr(wide),
                arr(channels, wide),
                arr(channels),
                arr(2 * channels, 2 * channels),
                arr(2 * channels),
                arr(channels, 2 * channels),
                arr(channels),
            ),
            in_specs=[vmem] * 4,
            out_specs=[vmem] * 12,
            compiler_params=pltpu.CompilerParams(vmem_limit_bytes=32 * 2**20),
        )(new_rows, grad_rows, slab, small)
    )
    return (
        new_rows.reshape(inputs.shape),
        grad_rows.reshape(inputs.shape),
        g_taps.transpose(1, 0, 2),
        g_gain,
        g_up,
        g_bup,
        g_down.T,
        g_bdown,
        g_gates,
        g_bgates,
        g_cand.T,
        g_bcand,
    )


def solution(mesh):
    field = P("tile", "date", None, None, None, None)
    return jax.shard_map(
        on_device,
        mesh=mesh,
        in_specs=(field,) * 3 + (P(),) * 11,
        out_specs=(field,) * 2 + (P(),) * 10,
        check_vma=False,
    )
```

time: 95.7 us -> 70.4 us (0.74)
  Pallas kernels: 81.2 us -> 65.5 us
  local copies, waits for them, and re-layouts: 10.7 us -> 3.93 us
  other arithmetic: 2.67 us -> 0 us
    pallas_call x1, Pallas kernels: 79.8 us -> 64.2 us  [on_device(): pl.pallas_call(functools.partial(level_kernel, side, x_low, norm_factor),...]
    unnamed x16 -> x8, local copies, waits for them, and re-layouts: 7.2 us -> 3.93 us
    another operation x7 -> x0, other arithmetic: 2.67 us -> none  [on_device(): jnp.stack([row(b_up), row(b_gates)] + [row(taps[axis, number]) for axis i...]
    slice x5 -> x0, local copies, waits for them, and re-layouts: 2.46 us -> none  [the longest x3 1.67 us: piece(): return flat[line * 128:line * 128 + size]]
where the time goes in v2:
time: 70.4 us; the launch traced here: 70.1 us
  Pallas kernels  65.5 us (93%)
  local copies, waits for them, and re-layouts  3.93 us (6%)
    pallas_call x1, Pallas kernels, on_device(): pl.pallas_call(functools.partial(level_kernel, side, x_low, norm_factor),...  64.2 us
    unnamed x8, local copies, waits for them, and re-layouts  3.93 us

profile of v2, /device:TPU:1, one launch (start us, length us, event | category | flops | bytes accessed | tf_op | source)
XLA Modules:
  0.0 70.1 jit_solution(5369167004910305090)
XLA Ops:
  0.6 64.2 %level.1 = (bf16[12,8,8,192]{3,2,1,0:T(8,128)(2,1)}, bf16[12,8,8,192]{3,2,1,0:T(8,128)(2,1)}, bf16[256,16,128]{2,1,0:T(8,128)(2,1)}, f32[32,128]{1,0:T(8,128)}) custom-call(s32[4,2,12]{2,1,0:T(2,128)} %bitcast.17, bf16[12,8,8,192]{3,2,1,0:T(8,128)(2,1)} %bitcast.12, bf16[12,8,8,192]{3,2,1,0:T(8,128)(2,1)} %bitcast.13, bf16[12,8,8,192]{3,2,1,0:T(8,128)(2,1)} %bitcast.14, ...), custom_call_target="tpu_custom_call" | custom-call | tf_op jit(solution)/shard_map/level/pallas_call | solution.py:816
  64.9 0.0 copy-start
  64.9 1.2 %copy-done = bf16[256,16,128]{2,1,0:T(8,128)(2,1)S(1)} copy-done((bf16[256,16,128]{2,1,0:T(8,128)(2,1)S(1)}, bf16[256,16,128]{2,1,0:T(8,128)(2,1)}, u32[]{:S(2)}) %copy-start) | copy-done | bytes 1048600
  66.1 0.0 copy-start.1
  66.1 1.0 %copy-done.1 = bf16[12,8,8,192]{3,2,1,0:T(8,128)(2,1)S(1)} copy-done((bf16[12,8,8,192]{3,2,1,0:T(8,128)(2,1)S(1)}, bf16[12,8,8,192]{3,2,1,0:T(8,128)(2,1)}, u32[]{:S(2)}) %copy-start.1) | copy-done | bytes 294936
  67.1 0.0 copy-start.2
  67.1 1.0 %copy-done.2 = bf16[12,8,8,192]{3,2,1,0:T(8,128)(2,1)S(1)} copy-done((bf16[12,8,8,192]{3,2,1,0:T(8,128)(2,1)S(1)}, bf16[12,8,8,192]{3,2,1,0:T(8,128)(2,1)}, u32[]{:S(2)}) %copy-start.2) | copy-done | bytes 294936
  68.1 0.0 copy-start.3
  68.1 0.7 %copy-done.3 = f32[32,128]{1,0:T(8,128)S(1)} copy-done((f32[32,128]{1,0:T(8,128)S(1)}, f32[32,128]{1,0:T(8,128)}, u32[]{:S(2)}) %copy-start.3) | copy-done | bytes 16408
  68.8 1.3 %unpack.1 = (bf16[12,8,8,192]{3,2,1,0:T(8,128)(2,1)}, bf16[12,8,8,192]{3,2,1,0:T(8,128)(2,1)}, bf16[3,2,192]{2,1,0:T(2,128)(2,1)}, bf16[192]{0:T(256)(128)(2,1)}...) custom-call(bf16[12,8,8,192]{3,2,1,0:T(8,128)(2,1)S(1)} %copy-done.1, ...), custom_call_target="tpu_custom_call" | custom-call | tf_op jit(solution)/shard_map/unpack/pallas_call | solution.py:903
Async XLA Ops:
  64.9 1.2 %copy-start = (bf16[256,16,128]{2,1,0:T(8,128)(2,1)S(1)}, bf16[256,16,128]{2,1,0:T(8,128)(2,1)}, u32[]{:S(2)}) copy-start(bf16[256,16,128]{2,1,0:T(8,128)(2,1)} %get-tuple-element.30.slab) | copy-start | bytes 3145732
  66.1 1.0 %copy-start.1 = (bf16[12,8,8,192]{3,2,1,0:T(8,128)(2,1)S(1)}, bf16[12,8,8,192]{3,2,1,0:T(8,128)(2,1)}, u32[]{:S(2)}) copy-start(bf16[12,8,8,192]{3,2,1,0:T(8,128)(2,1)} %get-tuple-element.28.ns) | copy-start | bytes 884740
  67.1 1.0 %copy-start.2 = (bf16[12,8,8,192]{3,2,1,0:T(8,128)(2,1)S(1)}, bf16[12,8,8,192]{3,2,1,0:T(8,128)(2,1)}, u32[]{:S(2)}) copy-start(bf16[12,8,8,192]{3,2,1,0:T(8,128)(2,1)} %get-tuple-element.29.gi) | copy-start | bytes 884740
  68.1 0.7 %copy-start.3 = (f32[32,128]{1,0:T(8,128)S(1)}, f32[32,128]{1,0:T(8,128)}, u32[]{:S(2)}) copy-start(f32[32,128]{1,0:T(8,128)} %get-tuple-element.31.small) | copy-start | bytes 49156

commit v3 on v2

--- a/solution.py
+++ b/solution.py
@@ -79,8 +79,16 @@
     w_cand_in,
     ns_out,
     gi_out,
-    slab_out,
-    small_out,
+    taps_out,
+    gain_out,
+    up_out,
+    b_up_out,
+    down_out,
+    b_down_out,
+    gates_out,
+    b_gates_out,
+    cand_out,
+    b_cand_out,
     adj,
     x_ref,
     h_ref,
@@ -98,6 +106,9 @@
     par,
     snd,
     rcv,
+    far_snd,
+    far_rcv,
+    far_pool,
     pool,
     halo,
     columns,
@@ -133,6 +144,8 @@
     load_sem,
     halo_send,
     halo_recv,
+    far_send,
+    far_recv,
     red_send,
     red_recv,
 ):
@@ -184,12 +197,6 @@
     @pl.when(has_across)
     def _():
         pl.semaphore_signal(barrier, inc=1, device_id=across, device_id_type=MESH)
-
-    peers = [offset(*step) for step in xy_steps]
-    peers += [offset(*step) for step in xz_steps if step[2]]
-    peers.append(sibling)
-    for peer in peers:
-        pl.semaphore_signal(barrier, inc=1, device_id=peer, device_id_type=MESH)
 
     loads = [
         pltpu.make_async_copy(src, dst, load_sem.at[number])
@@ -212,7 +219,13 @@
             )
         )
     ]
-    for load in loads:
+    loads[0].start()
+    peers = [offset(*step) for step in sorted(xy_steps, key=far)]
+    peers += [offset(*step) for step in sorted(xz_steps, key=far) if step[2]]
+    peers.append(sibling)
+    for peer in peers:
+        pl.semaphore_signal(barrier, inc=1, device_id=peer, device_id_type=MESH)
+    for load in loads[1:]:
         load.start()
 
     def tap(axis, number):
@@ -226,6 +239,9 @@
     def put_line(exchange, kind, value):
         snd[exchange, kind] = value.reshape(FACES * SIDE, channels).astype(BF16)
 
+    def rounded(value):
+        return value.astype(BF16).astype(F32)
+
     def put_columns(exchange):
         put_line(exchange, FIRST_COL, columns[0])
         put_line(exchange, LAST_COL, columns[1])
@@ -236,13 +252,21 @@
         return x_ref[:, pl.ds(i, 1)].astype(F32).reshape(FACES, SIDE, channels)
 
     def x_lines(i, carry):
-        set_columns(x_row(i), i)
+        value = x_row(i)
+        set_columns(value, i)
+        columns[2, :, pl.ds(i, 1), :] = value[:, 1:2, :]
+        columns[3, :, pl.ds(i, 1), :] = value[:, 6:7, :]
         return carry
 
     lax.fori_loop(0, 8, x_lines, 0)
     put_columns(0)
     put_line(0, FIRST_ROW, x_row(0))
     put_line(0, LAST_ROW, x_row(7))
+    for number, order in enumerate(((0, 2), (3, 1))):
+        for position, column in enumerate(order):
+            far_snd[number, position * 96 : position * 96 + 96] = (
+                columns[column].reshape(FACES * SIDE, channels).astype(BF16)
+            )
 
     @pl.when(has_across)
     def _():
@@ -251,16 +275,31 @@
     @pl.when(jnp.logical_not(has_across))
     def _():
         pl.semaphore_wait(barrier, len(peers))
+
+    row_first = jnp.logical_and(top, jnp.logical_not(west))
+    row_last = jnp.logical_and(bottom, jnp.logical_not(east))
+    col_first = jnp.logical_and(west, jnp.logical_not(top))
+    col_last = jnp.logical_and(east, jnp.logical_not(bottom))
+    corners = (jnp.logical_and(top, west), jnp.logical_and(bottom, east))
+
+    far_copies = [
+        pltpu.make_async_remote_copy(
+            src_ref=far_snd.at[number],
+            dst_ref=far_rcv.at[number],
+            send_sem=far_send.at[number],
+            recv_sem=far_recv.at[number],
+            device_id=across,
+            device_id_type=MESH,
+        )
+        for number in range(2)
+    ]
+    far_sends, far_receives = (col_first, col_last), (row_first, row_last)
 
     def halo_copies(exchange):
         on_columns = exchange in (0, 3)
         rows_turn = exchange in (0, 2)
         last, first = (LAST_COL, FIRST_COL) if on_columns else (LAST_ROW, FIRST_ROW)
         t_first, t_last = (FIRST_ROW, LAST_ROW) if rows_turn else (FIRST_COL, LAST_COL)
-        row_first = jnp.logical_and(top, jnp.logical_not(west))
-        row_last = jnp.logical_and(bottom, jnp.logical_not(east))
-        col_first = jnp.logical_and(west, jnp.logical_not(top))
-        col_last = jnp.logical_and(east, jnp.logical_not(bottom))
         if rows_turn:
             sends, receives = (row_first, row_last), (col_first, col_last)
         else:
@@ -285,6 +324,7 @@
                 line,
             )
             for kind, (line, target) in enumerate(zip((last, first, t_first, t_last), targets))
+            if kind < 2 or exchange != 1
         ]
 
     def start_halos(exchange):
@@ -303,7 +343,6 @@
 
     def receive_halos(exchange):
         copies = halo_copies(exchange)
-        corners = (jnp.logical_and(top, west), jnp.logical_and(bottom, east))
 
         def spread(ref, at):
             pool[at[0], at[1] : at[1] + 12] = (
@@ -338,6 +377,29 @@
                 index = jnp.where(jnp.logical_and(on_border, turned), 12 + neighbour, 24)
             to[face] = pool[which, index]
 
+    def border_lines(to, which, edge, on_border, row):
+        def spread(ref):
+            far_pool[which] = ref[...].astype(F32).reshape(2, FACES, SIDE, channels)
+
+        @pl.when(far_receives[which])
+        def _():
+            far_copies[which].wait_recv()
+            spread(far_rcv.at[which])
+
+        @pl.when(corners[which])
+        def _():
+            spread(far_snd.at[which])
+
+        own = x_row(row)
+        for face in range(FACES):
+            neighbour = adj[edge, 0, face]
+            turned = jnp.logical_and(on_border, adj[edge, 1, face] != (edge + 2) % 4)
+            straight = jnp.where(on_border, jnp.where(turned, 24, neighbour), face)
+            low, high = far_pool[which, 0, neighbour], far_pool[which, 1, neighbour]
+            lines = (own[face], low, high) if edge == 0 else (low, high, own[face])
+            made = sum(tap(0, number)[0] * lines[number] for number in range(3))
+            to[face] = jnp.where(turned, rounded(made), pool[which, straight])
+
     place = lax.broadcasted_iota(jnp.int32, (FACES, SIDE, channels), 1)
 
     def upright(which, i):
@@ -348,11 +410,11 @@
         right = jnp.where(place == 7, upright(east_lines, i), pltpu.roll(value, 7, 1))
         return left, right
 
-    def rounded(value):
-        return value.astype(BF16).astype(F32)
-
     start_halos(0)
+    for number in range(2):
+        pl.when(far_sends[number])(far_copies[number].start)
     pool[...] = jnp.zeros_like(pool)
+    far_pool[...] = jnp.zeros_like(far_pool)
     small[...] = jnp.zeros_like(small)
     slab[SMALL_AT : 2 * HALF] = jnp.zeros((2 * HALF - SMALL_AT, 16, 128), BF16)
     for load in loads[1:10]:
@@ -405,8 +467,8 @@
         @pl.when(b == 3)
         def _():
             receive_halos(1)
-            gather(field.at[0], 0, 0, top, "both")
-            gather(field.at[9], 1, 2, bottom, "both")
+            border_lines(field.at[0], 0, 0, top, 0)
+            border_lines(field.at[9], 1, 2, bottom, 7)
 
         def both(read):
             return jnp.concatenate(
@@ -428,11 +490,13 @@
         normed_s[rows, :] = normed
         pre = nn(normed, w_up[...]) + vector(ROW_BUP, 0, w_up.shape[1])
         square = pre * pre
-        curve = jnp.tanh(GELU_A * pre * (1.0 + GELU_B * square))
-        hid = (0.5 * pre * (1.0 + curve)).astype(BF16)
+        curve = jnp.tanh(pre * (GELU_A + (GELU_A * GELU_B) * square))
+        rise = 1.0 + curve
+        half = 0.5 * pre
+        hid = (half * rise).astype(BF16)
         hid_s[rows, :] = hid
-        slope = 0.5 * (1.0 + curve) + (0.5 * GELU_A) * pre * (1.0 - curve * curve) * (
-            1.0 + 3.0 * GELU_B * square
+        slope = rise * (
+            0.5 + half * (1.0 - curve) * (GELU_A + (3.0 * GELU_A * GELU_B) * square)
         )
         mixed = (
             both(row_of(x_ref)) + nt(hid, w_down_t[...]) + vector(ROW_BDOWN, 0, channels)
@@ -687,7 +751,23 @@
 
     small_z[tx] = sum_slots(small_y, 8).astype(BF16)
     spread_slot(small_z, tx, z_steps, 9)
-    small_out[...] = sum_slots(small_z, 9) * norm_factor
+    tile32[...] = sum_slots(small_z, 9) * norm_factor
+
+    def row_at(line, size):
+        pieces = [tile32[line + number : line + number + 1, :] for number in range(-(-size // 128))]
+        return jnp.concatenate(pieces, axis=1)[:, :size].astype(BF16)
+
+    for axis in range(2):
+        for number in range(3):
+            taps_out[number, axis : axis + 1, :] = row_at(9 + 2 * (3 * axis + number), channels)
+    for out, line in (
+        (b_up_out, 0),
+        (b_gates_out, 6),
+        (gain_out, 21),
+        (b_down_out, 23),
+        (b_cand_out, 25),
+    ):
+        out[...] = row_at(line, out.shape[0]).reshape(out.shape)
 
     def core_back(region):
         piece = gathered.at[pl.ds(base + region * REGION, REGION)]
@@ -699,10 +779,24 @@
         core_back(region).start()
     for region in range(2):
         core_back(region).wait_recv()
-    slab_out[...] = gathered[...]
+
+    def unpack(at, out):
+        columns_of_tiles = out.shape[1] // 128
+        for row in range(out.shape[0] // 16):
+            for column in range(columns_of_tiles):
+                out[row * 16 : row * 16 + 16, column * 128 : column * 128 + 128] = gathered[
+                    tile_place(at + row * columns_of_tiles + column)
+                ]
+
+    unpack(CAND_AT, cand_out)
+    unpack(GATES_AT, gates_out)
+    unpack(DOWN_AT, down_out)
+    unpack(UP_AT, up_out)
 
     for exchange in range(4):
         finish_halo_sends(exchange)
+    for number in range(2):
+        pl.when(far_sends[number])(far_copies[number].wait_send)
     small_core.wait_send()
     for region in range(2):
         core_copy(region).wait_send()
@@ -721,56 +815,17 @@
         whole_wait(ref, red_send.at[stage])
 
 
-def unpack_kernel(
-    ns,
-    gi,
-    slab,
-    small,
-    ns_out,
-    gi_out,
-    taps_out,
-    gain_out,
-    up_out,
-    b_up_out,
-    down_out,
-    b_down_out,
-    gates_out,
-    b_gates_out,
-    cand_out,
-    b_cand_out,
-):
-    ns_out[...] = ns[...]
-    gi_out[...] = gi[...]
-
-    def unpack(at, out):
-        across = out.shape[1] // 128
-        for row in range(out.shape[0] // 16):
-            for column in range(across):
-                out[row * 16 : row * 16 + 16, column * 128 : column * 128 + 128] = slab[
-                    tile_place(at + row * across + column)
-                ]
-
-    unpack(CAND_AT, cand_out)
-    unpack(GATES_AT, gates_out)
-    unpack(DOWN_AT, down_out)
-    unpack(UP_AT, up_out)
-
-    def row_at(line, size):
-        pieces = [small[line + number : line + number + 1, :] for number in range(-(-size // 128))]
-        return jnp.concatenate(pieces, axis=1)[:, :size].astype(BF16)
-
-    channels = gain_out.shape[0]
-    for axis in range(2):
-        for number in range(3):
-            taps_out[number, axis : axis + 1, :] = row_at(9 + 2 * (3 * axis + number), channels)
-    for out, line in (
-        (b_up_out, 0),
-        (b_gates_out, 6),
-        (gain_out, 21),
-        (b_down_out, 23),
-        (b_cand_out, 25),
-    ):
-        out[...] = row_at(line, out.shape[0]).reshape(out.shape)
+def relay_kernel(*refs):
+    count = (len(refs) - 1) // 2
+    sems = refs[-1]
+    copies = [
+        pltpu.make_async_copy(refs[number], refs[count + number], sems.at[number])
+        for number in range(count)
+    ]
+    for copy in copies:
+        copy.start()
+    for copy in copies:
+        copy.wait()
 
 
 def on_device(
@@ -813,17 +868,26 @@
         return jax.ShapeDtypeStruct(shape, BF16)
 
     shares = nx * side - 1
-    new_rows, grad_rows, slab, small = pl.pallas_call(
+    results = (
+        arr(*grid_shape),
+        arr(*grid_shape),
+        arr(3, 2, channels),
+        arr(channels),
+        arr(channels, wide),
+        arr(wide),
+        arr(channels, wide),
+        arr(channels),
+        arr(2 * channels, 2 * channels),
+        arr(2 * channels),
+        arr(channels, 2 * channels),
+        arr(channels),
+    )
+    made = pl.pallas_call(
         functools.partial(level_kernel, side, x_low, norm_factor),
         name="level",
-        out_shape=(
-            arr(*grid_shape),
-            arr(*grid_shape),
-            arr(2 * HALF, 16, 128),
-            jax.ShapeDtypeStruct((32, 128), F32),
-        ),
+        out_shape=results,
         in_specs=[hbm] * 14,
-        out_specs=[vmem] * 4,
+        out_specs=[vmem] * 12,
         scratch_shapes=[
             pltpu.SMEM((4, 2, FACES), jnp.int32),
             buf(*grid_shape),
@@ -842,9 +906,12 @@
             wide_buf(16, wide),
             buf(4, 4, lines, channels),
             buf(4, 4, lines, channels),
+            buf(2, 2 * lines, channels),
+            buf(2, 2 * lines, channels),
+            wide_buf(2, 2, FACES, SIDE, channels),
             wide_buf(2, 25, SIDE, channels),
             wide_buf(6, FACES, SIDE, channels),
-            wide_buf(2, FACES, SIDE, channels),
+            wide_buf(4, FACES, SIDE, channels),
             wide_buf(10, FACES, SIDE, channels),
             wide_buf(10, FACES, SIDE, channels),
             wide_buf(8, FACES, SIDE, channels),
@@ -877,6 +944,8 @@
             pltpu.SemaphoreType.DMA((14,)),
             pltpu.SemaphoreType.DMA((4, 4)),
             pltpu.SemaphoreType.DMA((4, 4)),
+            pltpu.SemaphoreType.DMA((2,)),
+            pltpu.SemaphoreType.DMA((2,)),
             pltpu.SemaphoreType.DMA((14,)),
             pltpu.SemaphoreType.DMA((14,)),
         ],
@@ -901,26 +970,14 @@
     )
     new_rows, grad_rows, g_taps, g_gain, g_up, g_bup, g_down, g_bdown, g_gates, g_bgates, g_cand, g_bcand = (
         pl.pallas_call(
-            unpack_kernel,
-            name="unpack",
-            out_shape=(
-                arr(*grid_shape),
-                arr(*grid_shape),
-                arr(3, 2, channels),
-                arr(channels),
-                arr(channels, wide),
-                arr(wide),
-                arr(channels, wide),
-                arr(channels),
-                arr(2 * channels, 2 * channels),
-                arr(2 * channels),
-                arr(channels, 2 * channels),
-                arr(channels),
-            ),
-            in_specs=[vmem] * 4,
-            out_specs=[vmem] * 12,
-            compiler_params=pltpu.CompilerParams(vmem_limit_bytes=32 * 2**20),
-        )(new_rows, grad_rows, slab, small)
+            relay_kernel,
+            name="relay",
+            out_shape=results,
+            in_specs=[hbm] * 12,
+            out_specs=[hbm] * 12,
+            scratch_shapes=[pltpu.SemaphoreType.DMA((12,))],
+            compiler_params=pltpu.CompilerParams(vmem_limit_bytes=60 * 2**20),
+        )(*made)
     )
     return (
         new_rows.reshape(inputs.shape),

time: 70.4 us -> 125 us (1.78)
  Pallas kernels: 65.5 us -> 124 us
  local copies, waits for them, and re-layouts: 3.93 us -> 0 us
    pallas_call x1, Pallas kernels: 1.29 us -> 56.5 us  [on_device(): pl.pallas_call(relay_kernel, name='relay', out_shape=results, in_specs=[h...]
    unnamed x8 -> x0, local copies, waits for them, and re-layouts: 3.93 us -> none
    pallas_call x1, Pallas kernels: 64.2 us -> 67.9 us  [on_device(): pl.pallas_call(functools.partial(level_kernel, side, x_low, norm_factor),...]
where the time goes in v3:
time: 125 us
  Pallas kernels  124 us (99%)
    pallas_call x1, Pallas kernels, on_device(): pl.pallas_call(functools.partial(level_kernel, side, x_low, norm_factor),...  67.9 us
    pallas_call x1, Pallas kernels, on_device(): pl.pallas_call(relay_kernel, name='relay', out_shape=results, in_specs=[h...  56.5 us

profile of v3, /device:TPU:1, one launch (start us, length us, event | category | flops | bytes accessed | tf_op | source)
XLA Modules:
  0.0 125.1 jit_solution(8871845633895291361)
XLA Ops:
  0.6 67.9 %level.1 = (bf16[12,8,8,192]{3,2,1,0:T(8,128)(2,1)}, bf16[12,8,8,192]{3,2,1,0:T(8,128)(2,1)}, bf16[3,2,192]{2,1,0:T(2,128)(2,1)}, bf16[192]{0:T(256)(128)(2,1)},...) custom-call(s32[4,2,12]{2,1,0:T(2,128)} %bitcast.17, ...), custom_call_target="tpu_custom_call" | custom-call | tf_op jit(solution)/shard_map/level/pallas_call | solution.py:885
  68.5 56.5 %relay.1 = (bf16[12,8,8,192]{3,2,1,0:T(8,128)(2,1)}, bf16[12,8,8,192]{3,2,1,0:T(8,128)(2,1)}, bf16[3,2,192]{2,1,0:T(2,128)(2,1)}, bf16[192]{0:T(256)(128)(2,1)},...) custom-call(bf16[12,8,8,192]{3,2,1,0:T(8,128)(2,1)} %get-tuple-eleme, ...), custom_call_target="tpu_custom_call" | custom-call | tf_op jit(solution)/shard_map/relay/pallas_call | solution.py:972

commit v4 on v3

--- a/solution.py
+++ b/solution.py
@@ -16,7 +16,8 @@
 SIDE = 8
 HALF = 128
 REGION = 64
-FIRST_ROW, LAST_ROW, FIRST_COL, LAST_COL = range(4)
+TURNED = 4
+ZERO_LINE = FACES + TURNED
 GELU_A = math.sqrt(2.0 / math.pi)
 GELU_B = 0.044715
 ROW_BUP, ROW_BGATES, ROW_TAPS, ROW_GAIN, ROW_BDOWN, ROW_BCAND = 0, 1, 2, 8, 9, 10
@@ -104,8 +105,11 @@
     w_gates,
     w_cand_t,
     par,
+    rank_of,
     snd,
     rcv,
+    turn_snd,
+    turn_rcv,
     far_snd,
     far_rcv,
     far_pool,
@@ -236,15 +240,22 @@
         columns[0, :, pl.ds(i, 1), :] = value[:, 0:1, :]
         columns[1, :, pl.ds(i, 1), :] = value[:, 7:8, :]
 
+    def rounded(value):
+        return value.astype(BF16).astype(F32)
+
     def put_line(exchange, kind, value):
         snd[exchange, kind] = value.reshape(FACES * SIDE, channels).astype(BF16)
 
-    def rounded(value):
-        return value.astype(BF16).astype(F32)
-
     def put_columns(exchange):
-        put_line(exchange, FIRST_COL, columns[0])
-        put_line(exchange, LAST_COL, columns[1])
+        put_line(exchange, 0, columns[1])
+        put_line(exchange, 1, columns[0])
+
+    def put_turned(ref, faces, line_of):
+        lines = [line_of(face).astype(F32) for face in faces]
+        ref[...] = jnp.concatenate(lines, axis=0).astype(BF16)
+
+    def is_turned(edge, face):
+        return adj[edge, 1, face] != (edge + 2) % 4
 
     loads[0].wait()
 
@@ -260,12 +271,31 @@
 
     lax.fori_loop(0, 8, x_lines, 0)
     put_columns(0)
-    put_line(0, FIRST_ROW, x_row(0))
-    put_line(0, LAST_ROW, x_row(7))
-    for number, order in enumerate(((0, 2), (3, 1))):
+
+    loads[2].wait()
+    turned_faces = []
+    for edge in range(4):
+        count = jnp.int32(0)
+        chosen = [jnp.int32(0)] * TURNED
+        for face in range(FACES):
+            rank_of[edge, face] = count
+            here = is_turned(edge, face)
+            chosen = [
+                jnp.where(jnp.logical_and(here, count == slot), face, old)
+                for slot, old in enumerate(chosen)
+            ]
+            count = count + jnp.where(here, 1, 0)
+        turned_faces.append(chosen)
+
+    put_turned(turn_snd.at[0, 0], turned_faces[0], lambda face: x_ref[face, 0])
+    put_turned(turn_snd.at[0, 1], turned_faces[2], lambda face: x_ref[face, 7])
+    for which, edge, order in ((0, 3, (0, 2)), (1, 1, (3, 1))):
         for position, column in enumerate(order):
-            far_snd[number, position * 96 : position * 96 + 96] = (
-                columns[column].reshape(FACES * SIDE, channels).astype(BF16)
+            part = pl.ds(position * TURNED * SIDE, TURNED * SIDE)
+            put_turned(
+                far_snd.at[which, part],
+                turned_faces[edge],
+                lambda face, column=column: columns[column, face],
             )
 
     @pl.when(has_across)
@@ -296,90 +326,90 @@
     far_sends, far_receives = (col_first, col_last), (row_first, row_last)
 
     def halo_copies(exchange):
-        on_columns = exchange in (0, 3)
-        rows_turn = exchange in (0, 2)
-        last, first = (LAST_COL, FIRST_COL) if on_columns else (LAST_ROW, FIRST_ROW)
-        t_first, t_last = (FIRST_ROW, LAST_ROW) if rows_turn else (FIRST_COL, LAST_COL)
-        if rows_turn:
+        if exchange in (0, 3):
+            ahead, behind = offset(0, 0, 1), offset(0, 0, side - 1)
+        else:
+            ahead, behind = offset(0, 1, 0), offset(0, side - 1, 0)
+        if exchange in (0, 2):
             sends, receives = (row_first, row_last), (col_first, col_last)
         else:
             sends, receives = (col_first, col_last), (row_first, row_last)
-        if on_columns:
-            ahead, behind = offset(0, 0, 1), offset(0, 0, side - 1)
-        else:
-            ahead, behind = offset(0, 1, 0), offset(0, side - 1, 0)
-        targets = (ahead, behind, across, across)
-        return [
-            (
-                pltpu.make_async_remote_copy(
-                    src_ref=snd.at[exchange, line],
-                    dst_ref=rcv.at[exchange, kind],
-                    send_sem=halo_send.at[exchange, kind],
-                    recv_sem=halo_recv.at[exchange, kind],
-                    device_id=target,
-                    device_id_type=MESH,
-                ),
-                None if kind < 2 else sends[kind - 2],
-                None if kind < 2 else receives[kind - 2],
-                line,
+        copies = []
+        for kind, target in enumerate((ahead, behind, across, across)):
+            turns = kind >= 2
+            if turns and exchange == 1:
+                continue
+            number = kind % 2
+            copy = pltpu.make_async_remote_copy(
+                src_ref=(turn_snd if turns else snd).at[exchange, number],
+                dst_ref=(turn_rcv if turns else rcv).at[exchange, number],
+                send_sem=halo_send.at[exchange, kind],
+                recv_sem=halo_recv.at[exchange, kind],
+                device_id=target,
+                device_id_type=MESH,
             )
-            for kind, (line, target) in enumerate(zip((last, first, t_first, t_last), targets))
-            if kind < 2 or exchange != 1
-        ]
+            copies.append(
+                (copy, sends[number] if turns else None, receives[number] if turns else None)
+            )
+        return copies
 
     def start_halos(exchange):
-        for copy, sends, _, _ in reversed(halo_copies(exchange)):
+        for copy, sends, _ in reversed(halo_copies(exchange)):
             if sends is None:
                 copy.start()
             else:
                 pl.when(sends)(copy.start)
 
     def finish_halo_sends(exchange):
-        for copy, sends, _, _ in halo_copies(exchange):
+        for copy, sends, _ in halo_copies(exchange):
             if sends is None:
                 copy.wait_send()
             else:
                 pl.when(sends)(copy.wait_send)
 
     def receive_halos(exchange):
-        copies = halo_copies(exchange)
-
-        def spread(ref, at):
-            pool[at[0], at[1] : at[1] + 12] = (
-                ref[...].astype(F32).reshape(FACES, SIDE, channels)
-            )
-
-        for kind, (copy, _, receives, line) in enumerate(copies):
+        for kind, (copy, _, receives) in enumerate(halo_copies(exchange)):
+            number = kind % 2
             if kind < 2:
                 copy.wait_recv()
-                spread(rcv.at[exchange, kind], (kind, 0))
-            else:
-
-                @pl.when(receives)
-                def _():
-                    copy.wait_recv()
-                    spread(rcv.at[exchange, kind], (kind - 2, 12))
-
-                @pl.when(corners[kind - 2])
-                def _():
-                    spread(snd.at[exchange, line], (kind - 2, 12))
+                pool[number, :FACES] = (
+                    rcv[exchange, number].astype(F32).reshape(FACES, SIDE, channels)
+                )
+                continue
+
+            def spread(ref):
+                pool[number, FACES:ZERO_LINE] = (
+                    ref[exchange, number].astype(F32).reshape(TURNED, SIDE, channels)
+                )
+
+            @pl.when(receives)
+            def _():
+                copy.wait_recv()
+                spread(turn_rcv)
+
+            @pl.when(corners[number])
+            def _():
+                spread(turn_snd)
 
     def gather(to, which, edge, on_border, mode):
         for face in range(FACES):
             neighbour = adj[edge, 0, face]
-            turned = adj[edge, 1, face] != (edge + 2) % 4
+            turned = is_turned(edge, face)
+            across_line = FACES + rank_of[3 - edge, neighbour]
             if mode == "both":
-                there = jnp.where(turned, 12 + neighbour, neighbour)
+                there = jnp.where(turned, across_line, neighbour)
                 index = jnp.where(on_border, there, face)
             elif mode == "straight":
-                index = jnp.where(on_border, jnp.where(turned, 24, neighbour), face)
+                index = jnp.where(on_border, jnp.where(turned, ZERO_LINE, neighbour), face)
             else:
-                index = jnp.where(jnp.logical_and(on_border, turned), 12 + neighbour, 24)
+                index = jnp.where(jnp.logical_and(on_border, turned), across_line, ZERO_LINE)
             to[face] = pool[which, index]
 
     def border_lines(to, which, edge, on_border, row):
         def spread(ref):
-            far_pool[which] = ref[...].astype(F32).reshape(2, FACES, SIDE, channels)
+            far_pool[which, :, :TURNED] = (
+                ref[...].astype(F32).reshape(2, TURNED, SIDE, channels)
+            )
 
         @pl.when(far_receives[which])
         def _():
@@ -393,9 +423,10 @@
         own = x_row(row)
         for face in range(FACES):
             neighbour = adj[edge, 0, face]
-            turned = jnp.logical_and(on_border, adj[edge, 1, face] != (edge + 2) % 4)
-            straight = jnp.where(on_border, jnp.where(turned, 24, neighbour), face)
-            low, high = far_pool[which, 0, neighbour], far_pool[which, 1, neighbour]
+            turned = jnp.logical_and(on_border, is_turned(edge, face))
+            straight = jnp.where(on_border, jnp.where(turned, ZERO_LINE, neighbour), face)
+            slot = rank_of[3 - edge, neighbour]
+            low, high = far_pool[which, 0, slot], far_pool[which, 1, slot]
             lines = (own[face], low, high) if edge == 0 else (low, high, own[face])
             made = sum(tap(0, number)[0] * lines[number] for number in range(3))
             to[face] = jnp.where(turned, rounded(made), pool[which, straight])
@@ -417,8 +448,8 @@
     far_pool[...] = jnp.zeros_like(far_pool)
     small[...] = jnp.zeros_like(small)
     slab[SMALL_AT : 2 * HALF] = jnp.zeros((2 * HALF - SMALL_AT, 16, 128), BF16)
-    for load in loads[1:10]:
-        load.wait()
+    for number in (1, 3, 4, 5, 6, 7, 8, 9):
+        loads[number].wait()
     for axis in range(2):
         for number in range(3):
             row = ROW_TAPS + 3 * axis + number
@@ -448,32 +479,18 @@
         left, right = column_shifts(value, 0, 1, i)
         first = rounded(tap(0, 0) * left + tap(0, 1) * value + tap(0, 2) * right)
         field[i + 1] = first
-        set_columns(first, i)
         return carry
 
     lax.fori_loop(0, 8, first_pass, 0)
-    put_columns(1)
-    put_line(1, FIRST_ROW, field[1])
-    put_line(1, LAST_ROW, field[8])
+    put_line(1, 0, field[8])
+    put_line(1, 1, field[1])
     start_halos(1)
 
     def vector(row, start, size):
         return par[row : row + 1, start : start + size]
 
-    def cell(b, sums):
-        rows = pl.ds(pl.multiple_of(b * 192, 192), 192)
-        pair = (2 * b + 1, lax.rem(2 * b + 2, 8))
-
-        @pl.when(b == 3)
-        def _():
-            receive_halos(1)
-            border_lines(field.at[0], 0, 0, top, 0)
-            border_lines(field.at[9], 1, 2, bottom, 7)
-
-        def both(read):
-            return jnp.concatenate(
-                [read(i).reshape(FACES * SIDE, channels) for i in pair], axis=0
-            )
+    def cell(blocks, sums):
+        gain = vector(ROW_GAIN, 0, channels)
 
         def second_row(i):
             return tap(1, 0) * field[i] + tap(1, 1) * field[i + 1] + tap(1, 2) * field[i + 2]
@@ -481,102 +498,151 @@
         def row_of(ref):
             return lambda i: ref[:, pl.ds(i, 1)].astype(F32)
 
-        gain = vector(ROW_GAIN, 0, channels)
-        centred = both(second_row)
-        centred = centred - jnp.mean(centred, axis=-1, keepdims=True)
-        inv_scale = lax.rsqrt(jnp.mean(centred * centred, axis=-1, keepdims=True) + EPSILON)
-        standard = centred * inv_scale
-        normed = (standard * gain).astype(BF16)
-        normed_s[rows, :] = normed
-        pre = nn(normed, w_up[...]) + vector(ROW_BUP, 0, w_up.shape[1])
-        square = pre * pre
-        curve = jnp.tanh(pre * (GELU_A + (GELU_A * GELU_B) * square))
-        rise = 1.0 + curve
-        half = 0.5 * pre
-        hid = (half * rise).astype(BF16)
-        hid_s[rows, :] = hid
-        slope = rise * (
-            0.5 + half * (1.0 - curve) * (GELU_A + (3.0 * GELU_A * GELU_B) * square)
-        )
-        mixed = (
-            both(row_of(x_ref)) + nt(hid, w_down_t[...]) + vector(ROW_BDOWN, 0, channels)
-        ).astype(BF16)
-        joined_s[rows, :channels] = mixed
-        prior = both(row_of(h_ref))
-        prior_b = prior.astype(BF16)
-        prior_s[rows, :] = prior_b
-        update = sigmoid(
-            nn(mixed, wg_u[:channels])
-            + nn(prior_b, wg_u[channels:])
-            + vector(ROW_BGATES, 0, channels)
-        )
-        reset = sigmoid(
-            nn(mixed, wg_r[:channels])
-            + nn(prior_b, wg_r[channels:])
-            + vector(ROW_BGATES, channels, channels)
-        )
-        reset_state = (reset * prior).astype(BF16)
-        joined_s[rows, channels:] = reset_state
-        candidate = jnp.tanh(
-            nt(mixed, wc_m[...]) + nt(reset_state, wc_r[...]) + vector(ROW_BCAND, 0, channels)
-        )
-        new = ((1.0 - update) * candidate + update * prior).astype(BF16)
-        upstream = both(row_of(g_ref))
-        kept = upstream * (1.0 - update)
-        d_cand = (kept * (1.0 - candidate * candidate)).astype(BF16)
-        d_cand_s[rows, :] = d_cand
-        d_update = (kept * (prior - candidate) * update).astype(BF16)
-        d_reset = (nn(d_cand, wc_r[...]) * prior * reset * (1.0 - reset)).astype(BF16)
-        d_gate_s[rows, :channels] = d_update
-        d_gate_s[rows, channels:] = d_reset
-        d_mixed = (
-            nn(d_cand, wc_m[...])
-            + nt(d_update, wg_u[:channels])
-            + nt(d_reset, wg_r[:channels])
-        ).astype(BF16)
-        d_mix_s[rows, :] = d_mixed
-        d_pre = (nn(d_mixed, w_down_t[...]) * slope).astype(BF16)
-        d_pre_s[rows, :] = d_pre
-        d_normed = nt(d_pre, w_up[...])
-        d_standard = d_normed * gain
-        d_second = rounded(
-            inv_scale
-            * (
-                d_standard
-                - jnp.mean(d_standard, axis=-1, keepdims=True)
-                - standard * jnp.mean(d_standard * standard, axis=-1, keepdims=True)
+        def joint(block, read):
+            parts = [read(i).reshape(FACES * SIDE, channels) for i in block[1]]
+            return parts[0] if len(parts) == 1 else jnp.concatenate(parts, axis=0)
+
+        def rows(block):
+            return pl.ds(pl.multiple_of(block[0] * 96, 96), 96 * len(block[1]))
+
+        states = [{"block": block} for block in blocks]
+
+        def norm(at):
+            centred = joint(at["block"], second_row)
+            centred = centred - jnp.mean(centred, axis=-1, keepdims=True)
+            at["inv"] = lax.rsqrt(jnp.mean(centred * centred, axis=-1, keepdims=True) + EPSILON)
+            at["standard"] = centred * at["inv"]
+            at["normed"] = (at["standard"] * gain).astype(BF16)
+            normed_s[rows(at["block"]), :] = at["normed"]
+
+        def up(at):
+            at["pre"] = nn(at["normed"], w_up[...]) + vector(ROW_BUP, 0, w_up.shape[1])
+
+        def bend(at):
+            pre = at["pre"]
+            square = pre * pre
+            curve = jnp.tanh(pre * (GELU_A + (GELU_A * GELU_B) * square))
+            rise = 1.0 + curve
+            half = 0.5 * pre
+            at["hid"] = (half * rise).astype(BF16)
+            hid_s[rows(at["block"]), :] = at["hid"]
+            at["slope"] = rise * (
+                0.5 + half * (1.0 - curve) * (GELU_A + (3.0 * GELU_A * GELU_B) * square)
             )
-        )
-        new = new.astype(F32)
-        for number, i in enumerate(pair):
-            part = slice(number * 96, number * 96 + 96)
-            d_sec[i + 1] = d_second[part].reshape(FACES, SIDE, channels)
-            ns_out[:, pl.ds(i, 1)] = (
-                new[part].reshape(FACES, 1, SIDE, channels).astype(BF16)
+
+        def down(at):
+            mixed = (
+                joint(at["block"], row_of(x_ref))
+                + nt(at["hid"], w_down_t[...])
+                + vector(ROW_BDOWN, 0, channels)
             )
+            at["mixed"] = mixed.astype(BF16)
+            joined_s[rows(at["block"]), :channels] = at["mixed"]
+
+        def gates(at):
+            mixed = at["mixed"]
+            at["prior"] = joint(at["block"], row_of(h_ref))
+            prior_b = at["prior"].astype(BF16)
+            prior_s[rows(at["block"]), :] = prior_b
+            at["reset"] = sigmoid(
+                nn(mixed, wg_r[:channels])
+                + nn(prior_b, wg_r[channels:])
+                + vector(ROW_BGATES, channels, channels)
+            )
+            at["update"] = sigmoid(
+                nn(mixed, wg_u[:channels])
+                + nn(prior_b, wg_u[channels:])
+                + vector(ROW_BGATES, 0, channels)
+            )
+
+        def propose(at):
+            reset_state = (at["reset"] * at["prior"]).astype(BF16)
+            joined_s[rows(at["block"]), channels:] = reset_state
+            at["candidate"] = jnp.tanh(
+                nt(at["mixed"], wc_m[...])
+                + nt(reset_state, wc_r[...])
+                + vector(ROW_BCAND, 0, channels)
+            )
+
+        def renew(at):
+            update, candidate, prior = at["update"], at["candidate"], at["prior"]
+            new = rounded((1.0 - update) * candidate + update * prior)
+            for number, i in enumerate(at["block"][1]):
+                ns_out[:, pl.ds(i, 1)] = (
+                    new[number * 96 : number * 96 + 96]
+                    .reshape(FACES, 1, SIDE, channels)
+                    .astype(BF16)
+                )
+            kept = joint(at["block"], row_of(g_ref)) * (1.0 - update)
+            at["d_cand"] = (kept * (1.0 - candidate * candidate)).astype(BF16)
+            d_cand_s[rows(at["block"]), :] = at["d_cand"]
+            at["d_update"] = (kept * (prior - candidate) * update).astype(BF16)
+            d_gate_s[rows(at["block"]), :channels] = at["d_update"]
+
+        def gates_back(at):
+            reset = at["reset"]
+            at["d_reset"] = (
+                nn(at["d_cand"], wc_r[...]) * at["prior"] * reset * (1.0 - reset)
+            ).astype(BF16)
+            d_gate_s[rows(at["block"]), channels:] = at["d_reset"]
+
+        def mixed_back(at):
+            at["d_mixed"] = (
+                nn(at["d_cand"], wc_m[...])
+                + nt(at["d_update"], wg_u[:channels])
+                + nt(at["d_reset"], wg_r[:channels])
+            ).astype(BF16)
+            d_mix_s[rows(at["block"]), :] = at["d_mixed"]
+
+        def hidden_back(at):
+            at["d_pre"] = (nn(at["d_mixed"], w_down_t[...]) * at["slope"]).astype(BF16)
+            d_pre_s[rows(at["block"]), :] = at["d_pre"]
+
+        def norm_back(at):
+            d_normed = nt(at["d_pre"], w_up[...])
+            standard = at["standard"]
+            d_standard = d_normed * gain
+            d_second = rounded(
+                at["inv"]
+                * (
+                    d_standard
+                    - jnp.mean(d_standard, axis=-1, keepdims=True)
+                    - standard * jnp.mean(d_standard * standard, axis=-1, keepdims=True)
+                )
+            )
+            for number, i in enumerate(at["block"][1]):
+                d_sec[i + 1] = d_second[number * 96 : number * 96 + 96].reshape(
+                    FACES, SIDE, channels
+                )
+            at["gain"] = d_normed * standard
+
+        for stage in (
+            norm, up, bend, down, gates, propose, renew, gates_back, mixed_back, hidden_back, norm_back,
+        ):
+            for at in states:
+                stage(at)
 
         def total(value):
             return jnp.sum(value.astype(F32), axis=0, keepdims=True)
 
-        extras = (
-            total(d_pre),
-            total(d_update),
-            total(d_reset),
-            total(d_normed * standard),
-            total(d_mixed),
-            total(d_cand),
-        )
-        return tuple(old + new_sum for old, new_sum in zip(sums, extras))
+        for at in states:
+            extras = [
+                total(at[name]) for name in ("d_pre", "d_update", "d_reset", "gain", "d_mixed", "d_cand")
+            ]
+            sums = tuple(old + extra for old, extra in zip(sums, extras))
+        return sums
 
     zeros = jnp.zeros((1, channels), F32)
-    sums = lax.fori_loop(
-        0,
-        4,
-        cell,
-        (jnp.zeros((1, w_up.shape[1]), F32), zeros, zeros, zeros, zeros, zeros),
-    )
-    put_line(2, FIRST_ROW, d_sec[1])
-    put_line(2, LAST_ROW, d_sec[8])
+    sums = (jnp.zeros((1, w_up.shape[1]), F32), zeros, zeros, zeros, zeros, zeros)
+    sums = cell([(0, (1, 2, 3, 4, 5, 6))], sums)
+    receive_halos(1)
+    border_lines(field.at[0], 0, 0, top, 0)
+    border_lines(field.at[9], 1, 2, bottom, 7)
+    sums = cell([(6, (7, 0))], sums)
+    put_line(2, 0, d_sec[8])
+    put_line(2, 1, d_sec[1])
+    put_turned(turn_snd.at[2, 0], turned_faces[0], lambda face: d_sec[1, face])
+    put_turned(turn_snd.at[2, 1], turned_faces[2], lambda face: d_sec[8, face])
     start_halos(2)
     small[ROW_BUP : ROW_BUP + 1, :] = sums[0]
     small[ROW_BGATES : ROW_BGATES + 1, :channels] = sums[1]
@@ -671,6 +737,8 @@
         0, 8, first_back, tuple(jnp.zeros((SIDE, channels), F32) for _ in range(6))
     )
     put_columns(3)
+    put_turned(turn_snd.at[3, 0], turned_faces[3], lambda face: columns[0, face])
+    put_turned(turn_snd.at[3, 1], turned_faces[1], lambda face: columns[1, face])
     start_halos(3)
 
     for number, tap_sum in enumerate(tap_sums):
@@ -815,16 +883,22 @@
         whole_wait(ref, red_send.at[stage])
 
 
-def relay_kernel(*refs):
-    count = (len(refs) - 1) // 2
-    sems = refs[-1]
-    copies = [
-        pltpu.make_async_copy(refs[number], refs[count + number], sems.at[number])
+def relay_kernel(count, *refs):
+    loads, stores = refs[3 * count :]
+    ins = [
+        pltpu.make_async_copy(refs[number], refs[2 * count + number], loads.at[number])
         for number in range(count)
     ]
-    for copy in copies:
+    outs = [
+        pltpu.make_async_copy(refs[2 * count + number], refs[count + number], stores.at[number])
+        for number in range(count)
+    ]
+    for copy in ins:
         copy.start()
-    for copy in copies:
+    for load, store in zip(ins, outs):
+        load.wait()
+        store.start()
+    for copy in outs:
         copy.wait()
 
 
@@ -904,12 +978,15 @@
             buf(2 * channels, 2 * channels),
             buf(channels, 2 * channels),
             wide_buf(16, wide),
-            buf(4, 4, lines, channels),
-            buf(4, 4, lines, channels),
-            buf(2, 2 * lines, channels),
-            buf(2, 2 * lines, channels),
-            wide_buf(2, 2, FACES, SIDE, channels),
-            wide_buf(2, 25, SIDE, channels),
+            pltpu.SMEM((4, FACES), jnp.int32),
+            buf(4, 2, lines, channels),
+            buf(4, 2, lines, channels),
+            buf(4, 2, TURNED * SIDE, channels),
+            buf(4, 2, TURNED * SIDE, channels),
+            buf(2, 2 * TURNED * SIDE, channels),
+            buf(2, 2 * TURNED * SIDE, channels),
+            wide_buf(2, 2, TURNED + 1, SIDE, channels),
+            wide_buf(2, ZERO_LINE + 1, SIDE, channels),
             wide_buf(6, FACES, SIDE, channels),
             wide_buf(4, FACES, SIDE, channels),
             wide_buf(10, FACES, SIDE, channels),
@@ -970,12 +1047,13 @@
     )
     new_rows, grad_rows, g_taps, g_gain, g_up, g_bup, g_down, g_bdown, g_gates, g_bgates, g_cand, g_bcand = (
         pl.pallas_call(
-            relay_kernel,
+            functools.partial(relay_kernel, len(results)),
             name="relay",
             out_shape=results,
             in_specs=[hbm] * 12,
             out_specs=[hbm] * 12,
-            scratch_shapes=[pltpu.SemaphoreType.DMA((12,))],
+            scratch_shapes=[buf(*result.shape) for result in results]
+            + [pltpu.SemaphoreType.DMA((12,))] * 2,
             compiler_params=pltpu.CompilerParams(vmem_limit_bytes=60 * 2**20),
         )(*made)
     )

time: 125 us -> 63.2 us (0.51)
  Pallas kernels: 124 us -> 62.4 us
    pallas_call x1, Pallas kernels: 56.5 us -> 2.45 us  [on_device(): pl.pallas_call(functools.partial(relay_kernel, len(results)), name='relay...]
    pallas_call x1, Pallas kernels: 67.9 us -> 59.9 us  [on_device(): pl.pallas_call(functools.partial(level_kernel, side, x_low, norm_factor),...]
where the time goes in v4:
time: 63.2 us; the launch traced here: 63 us
  Pallas kernels  62.4 us (99%)
  between operations  0.66 us (1%)
    pallas_call x1, Pallas kernels, on_device(): pl.pallas_call(functools.partial(level_kernel, side, x_low, norm_factor),...  59.9 us
    pallas_call x1, Pallas kernels, on_device(): pl.pallas_call(functools.partial(relay_kernel, len(results)), name='relay...  2.45 us

profile of v4, /device:TPU:1, one launch (start us, length us, event | category | flops | bytes accessed | tf_op | source)
XLA Modules:
  0.0 63.0 jit_solution(1500867892773363230)
XLA Ops:
  0.6 59.9 %level.1 = (bf16[12,8,8,192]{3,2,1,0:T(8,128)(2,1)}, bf16[12,8,8,192]{3,2,1,0:T(8,128)(2,1)}, bf16[3,2,192]{2,1,0:T(2,128)(2,1)}, bf16[192]{0:T(256)(128)(2,1)},...) custom-call(s32[4,2,12]{2,1,0:T(2,128)} %bitcast.17, ...), custom_call_target="tpu_custom_call" | custom-call | tf_op jit(solution)/shard_map/level/pallas_call | solution.py:959
  60.6 2.4 %relay.1 = (bf16[12,8,8,192]{3,2,1,0:T(8,128)(2,1)}, bf16[12,8,8,192]{3,2,1,0:T(8,128)(2,1)}, bf16[3,2,192]{2,1,0:T(2,128)(2,1)}, bf16[192]{0:T(256)(128)(2,1)},...) custom-call(bf16[12,8,8,192]{3,2,1,0:T(8,128)(2,1)} %get-tuple-eleme, ...), custom_call_target="tpu_custom_call" | custom-call | tf_op jit(solution)/shard_map/relay/pallas_call | solution.py:1049

commit v5 on v4

--- a/solution.py
+++ b/solution.py
@@ -166,14 +166,22 @@
     def device(x, y, z, c):
         return ((y * side + z) * 2 + lax.div(x, x_low), lax.rem(x, x_low) * 2 + c)
 
-    def moved(dx, dy, dz):
-        x = lax.rem(mx + dx, nx) if dx else mx
-        y = lax.rem(ty + dy, side) if dy else ty
-        z = lax.rem(tx + dz, side) if dz else tx
-        return x, y, z
+    x_at = [lax.rem(mx + step, nx) if step else mx for step in range(nx)]
+    y_at = [lax.rem(ty + step, side) if step else ty for step in range(side)]
+    z_at = [lax.rem(tx + step, side) if step else tx for step in range(side)]
+    x_tile = [lax.div(x, x_low) for x in x_at]
+    x_date = [lax.rem(x, x_low) * 2 + core for x in x_at]
+    y_tile = [y * (2 * side) for y in y_at]
+    z_tile = [z * 2 for z in z_at]
+    xy_tile = [[x + y for y in y_tile] for x in x_tile]
+    xz_tile = [[x + z for z in z_tile] for x in x_tile]
 
     def offset(dx, dy, dz):
-        return device(*moved(dx, dy, dz), core)
+        if not dz:
+            return xy_tile[dx][dy] + z_tile[0], x_date[dx]
+        if not dy:
+            return xz_tile[dx][dz] + y_tile[0], x_date[dx]
+        return x_tile[dx] + y_tile[dy] + z_tile[dz], x_date[dx]
 
     sibling = device(mx, ty, tx, 1 - core)
     across = device(mx, tx, ty, core)
@@ -489,7 +497,7 @@
     def vector(row, start, size):
         return par[row : row + 1, start : start + size]
 
-    def cell(blocks, sums):
+    def cell(blocks, sums, before_norm_back=None):
         gain = vector(ROW_GAIN, 0, channels)
 
         def second_row(i):
@@ -617,10 +625,14 @@
             at["gain"] = d_normed * standard
 
         for stage in (
-            norm, up, bend, down, gates, propose, renew, gates_back, mixed_back, hidden_back, norm_back,
+            norm, up, bend, down, gates, propose, renew, gates_back, mixed_back, hidden_back,
         ):
             for at in states:
                 stage(at)
+        if before_norm_back is not None:
+            before_norm_back()
+        for at in states:
+            norm_back(at)
 
         def total(value):
             return jnp.sum(value.astype(F32), axis=0, keepdims=True)
@@ -632,13 +644,43 @@
             sums = tuple(old + extra for old, extra in zip(sums, extras))
         return sums
 
+    def remote(src, dst, stage, target):
+        return pltpu.make_async_remote_copy(
+            src_ref=src,
+            dst_ref=dst,
+            send_sem=red_send.at[stage],
+            recv_sem=red_recv.at[stage],
+            device_id=target,
+            device_id_type=MESH,
+        )
+
+    def whole_wait(ref, sem):
+        pltpu.make_async_copy(ref, ref, sem).wait()
+
+    def core_copy(region):
+        return remote(
+            slab.at[pl.ds((1 - core) * HALF + region * REGION, REGION)],
+            core_rcv.at[pl.ds(region * REGION, REGION)],
+            region,
+            sibling,
+        )
+
+    def products():
+        store_tiles(slab, CAND_AT, tn(d_cand_s[...], joined_s[...]))
+        store_tiles(slab, GATES_AT, tn(joined_s[:, :channels], d_gate_s[...]))
+        store_tiles(slab, GATES_AT + 36, tn(prior_s[...], d_gate_s[...]))
+        store_tiles(slab, DOWN_AT, tn(d_mix_s[...], hid_s[...]))
+        core_copy(0).start()
+        store_tiles(slab, UP_AT, tn(normed_s[...], d_pre_s[...]))
+        core_copy(1).start()
+
     zeros = jnp.zeros((1, channels), F32)
     sums = (jnp.zeros((1, w_up.shape[1]), F32), zeros, zeros, zeros, zeros, zeros)
     sums = cell([(0, (1, 2, 3, 4, 5, 6))], sums)
     receive_halos(1)
     border_lines(field.at[0], 0, 0, top, 0)
     border_lines(field.at[9], 1, 2, bottom, 7)
-    sums = cell([(6, (7, 0))], sums)
+    sums = cell([(6, (7, 0))], sums, products)
     put_line(2, 0, d_sec[8])
     put_line(2, 1, d_sec[1])
     put_turned(turn_snd.at[2, 0], turned_faces[0], lambda face: d_sec[1, face])
@@ -651,35 +693,6 @@
     small[ROW_BDOWN : ROW_BDOWN + 1, :channels] = sums[4]
     small[ROW_BCAND : ROW_BCAND + 1, :channels] = sums[5]
 
-    def remote(src, dst, stage, target):
-        return pltpu.make_async_remote_copy(
-            src_ref=src,
-            dst_ref=dst,
-            send_sem=red_send.at[stage],
-            recv_sem=red_recv.at[stage],
-            device_id=target,
-            device_id_type=MESH,
-        )
-
-    def whole_wait(ref, sem):
-        pltpu.make_async_copy(ref, ref, sem).wait()
-
-    def core_copy(region):
-        return remote(
-            slab.at[pl.ds((1 - core) * HALF + region * REGION, REGION)],
-            core_rcv.at[pl.ds(region * REGION, REGION)],
-            region,
-            sibling,
-        )
-
-    store_tiles(slab, CAND_AT, tn(d_cand_s[...], joined_s[...]))
-    store_tiles(slab, GATES_AT, tn(joined_s[:, :channels], d_gate_s[...]))
-    store_tiles(slab, GATES_AT + 36, tn(prior_s[...], d_gate_s[...]))
-    store_tiles(slab, DOWN_AT, tn(d_mix_s[...], hid_s[...]))
-    core_copy(0).start()
-    store_tiles(slab, UP_AT, tn(normed_s[...], d_pre_s[...]))
-    core_copy(1).start()
-
     def add_cores(region):
         core_copy(region).wait_recv()
 
@@ -693,13 +706,13 @@
 
     def scatter(region, steps, received, stage):
         for number, step in enumerate(steps):
-            x, y, z = moved(*step)
-            other = z if region else y
+            dx, dy, dz = step
+            other = z_at[dz] if region else y_at[dy]
             remote(
-                t1.at[pl.ds(region * REGION + (x * side + other) * unit, unit)],
+                t1.at[pl.ds(region * REGION + (x_at[dx] * side + other) * unit, unit)],
                 received.at[number],
                 stage,
-                device(x, y, z, core),
+                offset(dx, dy, dz),
             ).start()
 
     add_cores(0)
@@ -884,21 +897,13 @@
 
 
 def relay_kernel(count, *refs):
-    loads, stores = refs[3 * count :]
-    ins = [
-        pltpu.make_async_copy(refs[number], refs[2 * count + number], loads.at[number])
+    copies = [
+        pltpu.make_async_copy(refs[number], refs[count + number], refs[-1].at[number])
         for number in range(count)
     ]
-    outs = [
-        pltpu.make_async_copy(refs[2 * count + number], refs[count + number], stores.at[number])
-        for number in range(count)
-    ]
-    for copy in ins:
+    for copy in copies:
         copy.start()
-    for load, store in zip(ins, outs):
-        load.wait()
-        store.start()
-    for copy in outs:
+    for copy in copies:
         copy.wait()
 
 
@@ -959,7 +964,7 @@
     made = pl.pallas_call(
         functools.partial(level_kernel, side, x_low, norm_factor),
         name="level",
-        out_shape=results,
+        out_shape=tuple(pltpu.VMEM(result.shape, result.dtype) for result in results),
         in_specs=[hbm] * 14,
         out_specs=[vmem] * 12,
         scratch_shapes=[
@@ -1050,11 +1055,10 @@
             functools.partial(relay_kernel, len(results)),
             name="relay",
             out_shape=results,
-            in_specs=[hbm] * 12,
+            in_specs=[vmem] * 12,
             out_specs=[hbm] * 12,
-            scratch_shapes=[buf(*result.shape) for result in results]
-            + [pltpu.SemaphoreType.DMA((12,))] * 2,
-            compiler_params=pltpu.CompilerParams(vmem_limit_bytes=60 * 2**20),
+            scratch_shapes=[pltpu.SemaphoreType.DMA((12,))],
+            compiler_params=pltpu.CompilerParams(vmem_limit_bytes=32 * 2**20),
         )(*made)
     )
     return (

time: 63.2 us -> 59.4 us (0.940)
  Pallas kernels: 62.4 us -> 58.6 us
    pallas_call x1, Pallas kernels: 59.9 us -> 57.3 us  [on_device(): pl.pallas_call(functools.partial(level_kernel, side, x_low, norm_factor),...]
    pallas_call x1, Pallas kernels: 2.45 us -> 1.35 us  [on_device(): pl.pallas_call(functools.partial(relay_kernel, len(results)), name='relay...]
where the time goes in v5:
time: 59.4 us; the launch traced here: 59.3 us
  Pallas kernels  58.6 us (99%)
  between operations  0.66 us (1%)
    pallas_call x1, Pallas kernels, on_device(): pl.pallas_call(functools.partial(level_kernel, side, x_low, norm_factor),...  57.3 us
    pallas_call x1, Pallas kernels, on_device(): pl.pallas_call(functools.partial(relay_kernel, len(results)), name='relay...  1.35 us

profile of v5, /device:TPU:1, one launch (start us, length us, event | category | flops | bytes accessed | tf_op | source)
XLA Modules:
  0.0 59.3 jit_solution(7486612806819821128)
XLA Ops:
  0.6 57.3 %level.1 = (bf16[12,8,8,192]{3,2,1,0:T(8,128)(2,1)S(1)}, bf16[12,8,8,192]{3,2,1,0:T(8,128)(2,1)S(1)}, bf16[3,2,192]{2,1,0:T(2,128)(2,1)S(1)}, bf16[192]{0:T(256)...) custom-call(s32[4,2,12]{2,1,0:T(2,128)} %bitcast.17, ...), custom_call_target="tpu_custom_call" | custom-call | tf_op jit(solution)/shard_map/level/pallas_call | solution.py:964
  57.9 1.4 %relay.1 = (bf16[12,8,8,192]{3,2,1,0:T(8,128)(2,1)}, bf16[12,8,8,192]{3,2,1,0:T(8,128)(2,1)}, bf16[3,2,192]{2,1,0:T(2,128)(2,1)}, bf16[192]{0:T(256)(128)(2,1)},...) custom-call(bf16[12,8,8,192]{3,2,1,0:T(8,128)(2,1)S(1)} %get-tuple-e, ...), custom_call_target="tpu_custom_call" | custom-call | tf_op jit(solution)/shard_map/relay/pallas_call | solution.py:1054

commit v6 on v5

--- a/solution.py
+++ b/solution.py
@@ -215,8 +215,8 @@
         for number, (src, dst) in enumerate(
             (
                 (x_in, x_ref),
+                (adj_in, adj),
                 (taps_in, taps_ref),
-                (adj_in, adj),
                 (w_gates_in, w_gates),
                 (w_cand_in, w_cand_t),
                 (gain_in, gain_ref),
@@ -232,12 +232,13 @@
         )
     ]
     loads[0].start()
+    loads[1].start()
     peers = [offset(*step) for step in sorted(xy_steps, key=far)]
     peers += [offset(*step) for step in sorted(xz_steps, key=far) if step[2]]
     peers.append(sibling)
     for peer in peers:
         pl.semaphore_signal(barrier, inc=1, device_id=peer, device_id_type=MESH)
-    for load in loads[1:]:
+    for load in loads[2:]:
         load.start()
 
     def tap(axis, number):
@@ -265,22 +266,7 @@
     def is_turned(edge, face):
         return adj[edge, 1, face] != (edge + 2) % 4
 
-    loads[0].wait()
-
-    def x_row(i):
-        return x_ref[:, pl.ds(i, 1)].astype(F32).reshape(FACES, SIDE, channels)
-
-    def x_lines(i, carry):
-        value = x_row(i)
-        set_columns(value, i)
-        columns[2, :, pl.ds(i, 1), :] = value[:, 1:2, :]
-        columns[3, :, pl.ds(i, 1), :] = value[:, 6:7, :]
-        return carry
-
-    lax.fori_loop(0, 8, x_lines, 0)
-    put_columns(0)
-
-    loads[2].wait()
+    loads[1].wait()
     turned_faces = []
     for edge in range(4):
         count = jnp.int32(0)
@@ -294,6 +280,21 @@
             ]
             count = count + jnp.where(here, 1, 0)
         turned_faces.append(chosen)
+
+    loads[0].wait()
+
+    def x_row(i):
+        return x_ref[:, pl.ds(i, 1)].astype(F32).reshape(FACES, SIDE, channels)
+
+    def x_lines(i, carry):
+        value = x_row(i)
+        set_columns(value, i)
+        columns[2, :, pl.ds(i, 1), :] = value[:, 1:2, :]
+        columns[3, :, pl.ds(i, 1), :] = value[:, 6:7, :]
+        return carry
+
+    lax.fori_loop(0, 8, x_lines, 0)
+    put_columns(0)
 
     put_turned(turn_snd.at[0, 0], turned_faces[0], lambda face: x_ref[face, 0])
     put_turned(turn_snd.at[0, 1], turned_faces[2], lambda face: x_ref[face, 7])
@@ -456,7 +457,7 @@
     far_pool[...] = jnp.zeros_like(far_pool)
     small[...] = jnp.zeros_like(small)
     slab[SMALL_AT : 2 * HALF] = jnp.zeros((2 * HALF - SMALL_AT, 16, 128), BF16)
-    for number in (1, 3, 4, 5, 6, 7, 8, 9):
+    for number in range(2, 10):
         loads[number].wait()
     for axis in range(2):
         for number in range(3):
@@ -497,7 +498,7 @@
     def vector(row, start, size):
         return par[row : row + 1, start : start + size]
 
-    def cell(blocks, sums, before_norm_back=None):
+    def cell(blocks, sums, hooks=None):
         gain = vector(ROW_GAIN, 0, channels)
 
         def second_row(i):
@@ -625,14 +626,12 @@
             at["gain"] = d_normed * standard
 
         for stage in (
-            norm, up, bend, down, gates, propose, renew, gates_back, mixed_back, hidden_back,
+            norm, up, bend, down, gates, propose, renew, gates_back, mixed_back, hidden_back, norm_back,
         ):
             for at in states:
                 stage(at)
-        if before_norm_back is not None:
-            before_norm_back()
-        for at in states:
-            norm_back(at)
+            if hooks and stage.__name__ in hooks:
+                hooks[stage.__name__]()
 
         def total(value):
             return jnp.sum(value.astype(F32), axis=0, keepdims=True)
@@ -665,14 +664,48 @@
             sibling,
         )
 
-    def products():
+    def add_cores(region):
+        core_copy(region).wait_recv()
+
+        def some(step, carry):
+            here = region * REGION + step * 8
+            total = slab[pl.ds(core * HALF + here, 8)].astype(F32)
+            t1[pl.ds(here, 8)] = (total + core_rcv[pl.ds(here, 8)].astype(F32)).astype(BF16)
+            return carry
+
+        lax.fori_loop(0, REGION // 8, some, 0)
+
+    def scatter(region, steps, received, stage):
+        for number, step in enumerate(steps):
+            dx, dy, dz = step
+            other = z_at[dz] if region else y_at[dy]
+            remote(
+                t1.at[pl.ds(region * REGION + (x_at[dx] * side + other) * unit, unit)],
+                received.at[number],
+                stage,
+                offset(dx, dy, dz),
+            ).start()
+
+    def early_products():
         store_tiles(slab, CAND_AT, tn(d_cand_s[...], joined_s[...]))
         store_tiles(slab, GATES_AT, tn(joined_s[:, :channels], d_gate_s[...]))
         store_tiles(slab, GATES_AT + 36, tn(prior_s[...], d_gate_s[...]))
+
+    def down_product():
         store_tiles(slab, DOWN_AT, tn(d_mix_s[...], hid_s[...]))
         core_copy(0).start()
+
+    def up_product():
         store_tiles(slab, UP_AT, tn(normed_s[...], d_pre_s[...]))
         core_copy(1).start()
+        add_cores(0)
+        scatter(0, xy_steps, xy_rcv, 2)
+
+    hooks = {
+        "gates_back": early_products,
+        "mixed_back": down_product,
+        "hidden_back": up_product,
+    }
 
     zeros = jnp.zeros((1, channels), F32)
     sums = (jnp.zeros((1, w_up.shape[1]), F32), zeros, zeros, zeros, zeros, zeros)
@@ -680,7 +713,7 @@
     receive_halos(1)
     border_lines(field.at[0], 0, 0, top, 0)
     border_lines(field.at[9], 1, 2, bottom, 7)
-    sums = cell([(6, (7, 0))], sums, products)
+    sums = cell([(6, (7, 0))], sums, hooks)
     put_line(2, 0, d_sec[8])
     put_line(2, 1, d_sec[1])
     put_turned(turn_snd.at[2, 0], turned_faces[0], lambda face: d_sec[1, face])
@@ -693,30 +726,6 @@
     small[ROW_BDOWN : ROW_BDOWN + 1, :channels] = sums[4]
     small[ROW_BCAND : ROW_BCAND + 1, :channels] = sums[5]
 
-    def add_cores(region):
-        core_copy(region).wait_recv()
-
-        def some(step, carry):
-            here = region * REGION + step * 8
-            total = slab[pl.ds(core * HALF + here, 8)].astype(F32)
-            t1[pl.ds(here, 8)] = (total + core_rcv[pl.ds(here, 8)].astype(F32)).astype(BF16)
-            return carry
-
-        lax.fori_loop(0, REGION // 8, some, 0)
-
-    def scatter(region, steps, received, stage):
-        for number, step in enumerate(steps):
-            dx, dy, dz = step
-            other = z_at[dz] if region else y_at[dy]
-            remote(
-                t1.at[pl.ds(region * REGION + (x_at[dx] * side + other) * unit, unit)],
-                received.at[number],
-                stage,
-                offset(dx, dy, dz),
-            ).start()
-
-    add_cores(0)
-    scatter(0, xy_steps, xy_rcv, 2)
     add_cores(1)
     scatter(1, xz_steps, xz_rcv, 3)
 
@@ -832,6 +841,14 @@
 
     small_z[tx] = sum_slots(small_y, 8).astype(BF16)
     spread_slot(small_z, tx, z_steps, 9)
+    def core_back(region):
+        piece = gathered.at[pl.ds(base + region * REGION, REGION)]
+        return remote(piece, piece, 12 + region, sibling)
+
+    shares = nx * side - 1
+    for region in range(2):
+        whole_wait(gathered.at[pl.ds(0, unit * shares)], red_recv.at[10 + region])
+        core_back(region).start()
     tile32[...] = sum_slots(small_z, 9) * norm_factor
 
     def row_at(line, size):
@@ -850,14 +867,6 @@
     ):
         out[...] = row_at(line, out.shape[0]).reshape(out.shape)
 
-    def core_back(region):
-        piece = gathered.at[pl.ds(base + region * REGION, REGION)]
-        return remote(piece, piece, 12 + region, sibling)
-
-    shares = nx * side - 1
-    for region in range(2):
-        whole_wait(gathered.at[pl.ds(0, unit * shares)], red_recv.at[10 + region])
-        core_back(region).start()
     for region in range(2):
         core_back(region).wait_recv()
 

time: 59.4 us -> 62.1 us (1.045)
  Pallas kernels: 58.6 us -> 61.3 us
    pallas_call x1, Pallas kernels: 57.3 us -> 60 us  [on_device(): pl.pallas_call(functools.partial(level_kernel, side, x_low, norm_factor),...]
where the time goes in v6:
time: 62.1 us; the launch traced here: 62 us
  Pallas kernels  61.3 us (99%)
  between operations  0.66 us (1%)
    pallas_call x1, Pallas kernels, on_device(): pl.pallas_call(functools.partial(level_kernel, side, x_low, norm_factor),...  60 us
    pallas_call x1, Pallas kernels, on_device(): pl.pallas_call(functools.partial(relay_kernel, len(results)), name='relay...  1.35 us

profile of v6, /device:TPU:1, one launch (start us, length us, event | category | flops | bytes accessed | tf_op | source)
XLA Modules:
  0.0 62.0 jit_solution(9394806289645119184)
XLA Ops:
  0.6 60.0 %level.1 = (bf16[12,8,8,192]{3,2,1,0:T(8,128)(2,1)S(1)}, bf16[12,8,8,192]{3,2,1,0:T(8,128)(2,1)S(1)}, bf16[3,2,192]{2,1,0:T(2,128)(2,1)S(1)}, bf16[192]{0:T(256)...) custom-call(s32[4,2,12]{2,1,0:T(2,128)} %bitcast.17, ...), custom_call_target="tpu_custom_call" | custom-call | tf_op jit(solution)/shard_map/level/pallas_call | solution.py:973
  60.6 1.4 %relay.1 = (bf16[12,8,8,192]{3,2,1,0:T(8,128)(2,1)}, bf16[12,8,8,192]{3,2,1,0:T(8,128)(2,1)}, bf16[3,2,192]{2,1,0:T(2,128)(2,1)}, bf16[192]{0:T(256)(128)(2,1)},...) custom-call(bf16[12,8,8,192]{3,2,1,0:T(8,128)(2,1)S(1)} %get-tuple-e, ...), custom_call_target="tpu_custom_call" | custom-call | tf_op jit(solution)/shard_map/relay/pallas_call | solution.py:1063

commit v7 on v5

--- a/solution.py
+++ b/solution.py
@@ -215,8 +215,8 @@
         for number, (src, dst) in enumerate(
             (
                 (x_in, x_ref),
+                (adj_in, adj),
                 (taps_in, taps_ref),
-                (adj_in, adj),
                 (w_gates_in, w_gates),
                 (w_cand_in, w_cand_t),
                 (gain_in, gain_ref),
@@ -232,12 +232,13 @@
         )
     ]
     loads[0].start()
+    loads[1].start()
     peers = [offset(*step) for step in sorted(xy_steps, key=far)]
     peers += [offset(*step) for step in sorted(xz_steps, key=far) if step[2]]
     peers.append(sibling)
     for peer in peers:
         pl.semaphore_signal(barrier, inc=1, device_id=peer, device_id_type=MESH)
-    for load in loads[1:]:
+    for load in loads[2:]:
         load.start()
 
     def tap(axis, number):
@@ -265,22 +266,7 @@
     def is_turned(edge, face):
         return adj[edge, 1, face] != (edge + 2) % 4
 
-    loads[0].wait()
-
-    def x_row(i):
-        return x_ref[:, pl.ds(i, 1)].astype(F32).reshape(FACES, SIDE, channels)
-
-    def x_lines(i, carry):
-        value = x_row(i)
-        set_columns(value, i)
-        columns[2, :, pl.ds(i, 1), :] = value[:, 1:2, :]
-        columns[3, :, pl.ds(i, 1), :] = value[:, 6:7, :]
-        return carry
-
-    lax.fori_loop(0, 8, x_lines, 0)
-    put_columns(0)
-
-    loads[2].wait()
+    loads[1].wait()
     turned_faces = []
     for edge in range(4):
         count = jnp.int32(0)
@@ -294,6 +280,21 @@
             ]
             count = count + jnp.where(here, 1, 0)
         turned_faces.append(chosen)
+
+    loads[0].wait()
+
+    def x_row(i):
+        return x_ref[:, pl.ds(i, 1)].astype(F32).reshape(FACES, SIDE, channels)
+
+    def x_lines(i, carry):
+        value = x_row(i)
+        set_columns(value, i)
+        columns[2, :, pl.ds(i, 1), :] = value[:, 1:2, :]
+        columns[3, :, pl.ds(i, 1), :] = value[:, 6:7, :]
+        return carry
+
+    lax.fori_loop(0, 8, x_lines, 0)
+    put_columns(0)
 
     put_turned(turn_snd.at[0, 0], turned_faces[0], lambda face: x_ref[face, 0])
     put_turned(turn_snd.at[0, 1], turned_faces[2], lambda face: x_ref[face, 7])
@@ -456,7 +457,7 @@
     far_pool[...] = jnp.zeros_like(far_pool)
     small[...] = jnp.zeros_like(small)
     slab[SMALL_AT : 2 * HALF] = jnp.zeros((2 * HALF - SMALL_AT, 16, 128), BF16)
-    for number in (1, 3, 4, 5, 6, 7, 8, 9):
+    for number in range(2, 10):
         loads[number].wait()
     for axis in range(2):
         for number in range(3):
@@ -832,6 +833,14 @@
 
     small_z[tx] = sum_slots(small_y, 8).astype(BF16)
     spread_slot(small_z, tx, z_steps, 9)
+    def core_back(region):
+        piece = gathered.at[pl.ds(base + region * REGION, REGION)]
+        return remote(piece, piece, 12 + region, sibling)
+
+    shares = nx * side - 1
+    for region in range(2):
+        whole_wait(gathered.at[pl.ds(0, unit * shares)], red_recv.at[10 + region])
+        core_back(region).start()
     tile32[...] = sum_slots(small_z, 9) * norm_factor
 
     def row_at(line, size):
@@ -850,14 +859,6 @@
     ):
         out[...] = row_at(line, out.shape[0]).reshape(out.shape)
 
-    def core_back(region):
-        piece = gathered.at[pl.ds(base + region * REGION, REGION)]
-        return remote(piece, piece, 12 + region, sibling)
-
-    shares = nx * side - 1
-    for region in range(2):
-        whole_wait(gathered.at[pl.ds(0, unit * shares)], red_recv.at[10 + region])
-        core_back(region).start()
     for region in range(2):
         core_back(region).wait_recv()
 

time: 59.4 us -> 58.3 us (0.981)
  Pallas kernels: 58.6 us -> 57.6 us
    pallas_call x1, Pallas kernels: 57.3 us -> 56.2 us  [on_device(): pl.pallas_call(functools.partial(level_kernel, side, x_low, norm_factor),...]
where the time goes in v7:
time: 58.3 us; the launch traced here: 58.2 us
  Pallas kernels  57.6 us (99%)
  between operations  0.66 us (1%)
    pallas_call x1, Pallas kernels, on_device(): pl.pallas_call(functools.partial(level_kernel, side, x_low, norm_factor),...  56.2 us
    pallas_call x1, Pallas kernels, on_device(): pl.pallas_call(functools.partial(relay_kernel, len(results)), name='relay...  1.35 us

profile of v7, /device:TPU:1, one launch (start us, length us, event | category | flops | bytes accessed | tf_op | source)
XLA Modules:
  0.0 58.2 jit_solution(4451429047513098792)
XLA Ops:
  0.6 56.2 %level.1 = (bf16[12,8,8,192]{3,2,1,0:T(8,128)(2,1)S(1)}, bf16[12,8,8,192]{3,2,1,0:T(8,128)(2,1)S(1)}, bf16[3,2,192]{2,1,0:T(2,128)(2,1)S(1)}, bf16[192]{0:T(256)...) custom-call(s32[4,2,12]{2,1,0:T(2,128)} %bitcast.17, ...), custom_call_target="tpu_custom_call" | custom-call | tf_op jit(solution)/shard_map/level/pallas_call | solution.py:965
  56.9 1.4 %relay.1 = (bf16[12,8,8,192]{3,2,1,0:T(8,128)(2,1)}, bf16[12,8,8,192]{3,2,1,0:T(8,128)(2,1)}, bf16[3,2,192]{2,1,0:T(2,128)(2,1)}, bf16[192]{0:T(256)(128)(2,1)},...) custom-call(bf16[12,8,8,192]{3,2,1,0:T(8,128)(2,1)S(1)} %get-tuple-e, ...), custom_call_target="tpu_custom_call" | custom-call | tf_op jit(solution)/shard_map/relay/pallas_call | solution.py:1055
